TPU v7x, 1024 devices: a whole 4x8x16 slice. The times are simulated.
1024 devices in a mesh: batch: 64 (over z, x), proto: 16 (over y, core).
Axes of the slice: x: 4, y: 8, z: 16, core: 2. Of those that a mesh axis runs over, the one named last changes fastest.
Arguments:
- student_feat: bfloat16 [10240, 128], P('batch'), may hold values from -6 to 6
- teacher_feat: bfloat16 [2048, 128], P('batch'), may hold values from -6 to 6
- prototypes: float32 [128, 65536], P(None, 'proto'), may hold values from -0.12 to 0.12
- crop_image: int32 [10240], P('batch'), may hold values from 0 to 1023, as said below
- crop_kind: int32 [10240], P('batch'), may hold values from 0 to 2, as said below
Outputs:
- grad_proto: float32 [128, 65536], P('batch', 'proto')
- grad_student: float32 [10240, 128], P('batch')
Inputs may be any that keep to these rules, and one draw needn't show every extreme that they name: `crop_image`: the rows of one device (aligned blocks of 160 rows, block j) name the images j * 16 to (j + 1) * 16 - 1, each exactly 10 times, in an order drawn from the seed. `crop_kind`: each image has exactly one crop of kind 1, one of kind 2 and 8 of kind 0.
All inputs are finite; a program needn't handle non-finite values.
Results may differ from a plain program's by a relative error of at most 0.0033.
Values sent between devices are 32-bit elements; how exact they have to be, the bound alone decides.
No kernel may reach another device: no remote copies, remote signals or barrier semaphores. Data moves between devices by JAX's collectives and lax.ppermute only.
A program may use at most 32 MiB of HBM per device.

v0:
```python
import jax
import jax.numpy as jnp
from jax import lax
from jax.sharding import PartitionSpec as P

ITERS = 3
LOSS_SCALE = 16


EPS = 1e-06
TEACH_TEMP = 0.04
STUD_TEMP = 0.1


def row_unit(x):
    norm = jnp.sqrt(jnp.sum(x * x, axis=-1, keepdims=True) + EPS)
    return (x / norm, norm)


def per_device(student_feat, teacher_feat, prototypes, crop_image, crop_kind):
    vnorm = jnp.sqrt(jnp.sum(prototypes * prototypes, axis=0) + EPS)
    unit = prototypes / vnorm[None, :]
    unit_half = unit.astype(jnp.bfloat16)
    s_unit, s_norm = row_unit(student_feat.astype(jnp.float32))
    s_half = s_unit.astype(jnp.bfloat16)
    t_unit = row_unit(teacher_feat.astype(jnp.float32))[0]
    t_half = t_unit.astype(jnp.bfloat16)
    expo = jnp.exp(jnp.dot(t_half, unit_half, preferred_element_type=jnp.float32) / TEACH_TEMP)
    logits = jnp.dot(s_half, unit_half, preferred_element_type=jnp.float32)
    s_part = jnp.sum(jnp.exp(logits / STUD_TEMP), axis=1)
    s_total = lax.psum(s_part, "proto")
    teach_rows = teacher_feat.shape[0]
    scale_a = jnp.ones((teach_rows,), jnp.float32)
    for step in range(ITERS):
        column = lax.psum(jnp.sum(scale_a[:, None] * expo, axis=0), "batch")
        scale_b = 1.0 / column
        row_part = jnp.sum(expo * scale_b[None, :], axis=1)
        if step < ITERS - 1:
            row_total = lax.psum(row_part, "proto")
        else:
            row_total = lax.psum(row_part, "proto")
        scale_a = 1.0 / row_total
    target_q = scale_a[:, None] * expo * scale_b[None, :]
    prob = jnp.exp(logits / STUD_TEMP) / s_total[:, None]
    base = lax.axis_index("batch") * (teach_rows // 2)
    local_image = crop_image - base
    teach_index = lax.iota(jnp.int32, teach_rows)
    teach_image = teach_index // 2
    teach_view = teach_index % 2
    kcol = crop_kind[:, None]
    matches = local_image[:, None] == teach_image[None, :]
    weighting = jnp.where(kcol == 0, 0.5, jnp.where(teach_view[None, :] == 2 - kcol, 1.0, 0.0))
    selector = jnp.where(matches, weighting, 0.0).astype(jnp.float32)
    target = jnp.dot(selector, target_q, precision=lax.Precision.HIGHEST)
    dlogit = (LOSS_SCALE / STUD_TEMP * (prob - target)).astype(jnp.bfloat16)
    dz_part = lax.dot_general(
        dlogit, unit_half, (((1,), (1,)), ((), ())), preferred_element_type=jnp.float32
    )
    dz = lax.psum(dz_part, "proto")
    grad_student = (dz - s_unit * jnp.sum(s_unit * dz, axis=1, keepdims=True)) / s_norm
    bot = prototypes.shape[0]
    own_rows = bot // lax.axis_size("batch")
    start_row = lax.axis_index("batch") * own_rows
    unit_mine = lax.dynamic_slice_in_dim(unit, start_row, own_rows, 0)
    partial_grad = lax.dot_general(
        s_half, dlogit, (((0,), (0,)), ((), ())), preferred_element_type=jnp.float32
    )
    dunit = lax.psum_scatter(partial_grad, "batch", scatter_dimension=0, tiled=True)
    half_mine = lax.dynamic_slice_in_dim(unit_half, start_row, own_rows, 0).astype(jnp.float32)
    dots = lax.psum(jnp.sum(half_mine * dunit, axis=0), "batch")
    grad_proto = (dunit - unit_mine * dots[None, :]) / vnorm[None, :]
    return (grad_proto, grad_student)


def solution(mesh):
    return jax.shard_map(
        per_device,
        mesh=mesh,
        in_specs=(P("batch", None), P("batch", None), P(None, "proto"), P("batch"), P("batch")),
        out_specs=(P("batch", "proto"), P("batch", None)),
        check_vma=False,
    )
```

profile of v0, /device:TPU:8, one launch (start us, length us, event | category | flops | bytes accessed | tf_op | source)
XLA Modules:
  0.0 1619.8 jit_solution(9835066378485582803)
XLA Ops:
  7.2 0.0 all-reduce.5.cloned.1.call-start
  7.2 0.0 copy-start
  7.2 1.9 multiply_reduce_fusion
  9.2 0.3 copy-done
  9.4 0.0 copy-start.2
  9.4 1.7 fusion.32
  11.1 0.0 copy-done.2
  11.1 0.1 fusion.25
  11.3 0.0 copy-start.1
  11.3 0.4 fusion.34
  11.6 292.4 %psum.64 = f32[4096]{0:T(1024)S(1)} all-reduce(f32[4096]{0:T(1024)S(1)} %get-tuple-element.8), channel_id=1, replica_groups=mesh['batch'=64,'proto'=16] {'batch'}, use_global_device_ids=true, to_apply=%region_6.0 | all-reduce | flops 4096 | bytes 32768 | tf_op jit(solution)/shard_map/psum | solution.py:35
  304.1 0.2 multiply_reduce_fusion.5
  304.3 20.7 %psum.65 = f32[32]{0:T(128)S(1)} all-reduce(f32[32]{0:T(128)S(1)} %multiply_reduce_fusion.5), channel_id=1, replica_groups=mesh['batch'=64,'proto'=16] {'proto'}, use_global_device_ids=true, to_apply=%region_8.0 | all-reduce | flops 32 | bytes 256 | tf_op jit(solution)/shard_map/psum | solution.py:39
  324.9 0.1 multiply_reduce_fusion.4
  325.1 274.0 %psum.66 = f32[4096]{0:T(1024)S(1)} all-reduce(f32[4096]{0:T(1024)S(1)} %multiply_reduce_fusion.4), channel_id=1, replica_groups=mesh['batch'=64,'proto'=16] {'batch'}, use_global_device_ids=true, to_apply=%region_10.0 | all-reduce | flops 4096 | bytes 32768 | tf_op jit(solution)/shard_map/psum | solution.py:35
  599.0 0.2 multiply_reduce_fusion.3
  599.2 23.5 %psum.67 = f32[32]{0:T(128)S(1)} all-reduce(f32[32]{0:T(128)S(1)} %multiply_reduce_fusion.3), channel_id=1, replica_groups=mesh['batch'=64,'proto'=16] {'proto'}, use_global_device_ids=true, to_apply=%region_12.0 | all-reduce | flops 32 | bytes 256 | tf_op jit(solution)/shard_map/psum | solution.py:39
  622.8 0.1 multiply_reduce_fusion.2
  622.9 274.0 %psum.68 = f32[4096]{0:T(1024)S(1)} all-reduce(f32[4096]{0:T(1024)S(1)} %multiply_reduce_fusion.2), channel_id=1, replica_groups=mesh['batch'=64,'proto'=16] {'batch'}, use_global_device_ids=true, to_apply=%region_14.0 | all-reduce | flops 4096 | bytes 32768 | tf_op jit(solution)/shard_map/psum | solution.py:35
  896.9 0.0 copy-start.3
  896.9 0.0 copy-start.4
  896.9 0.2 multiply_reduce_fusion.1
  897.0 0.0 copy-done.1
  897.0 0.1 fusion.8
  897.2 2.1 fusion.33
  899.2 23.5 %all-reduce.1 = (f32[160]{0:T(256)S(1)}, f32[32]{0:T(128)S(1)}) all-reduce(f32[160]{0:T(256)S(1)} %get-tuple-element.6, f32[32]{0:T(128)S(1)} %multiply_reduce_fusion.1), channel_id=1, replica_groups=mesh['batch'=64,'proto'=16] {'proto'}, use_global_device_ids=true, to_apply=%region_3.0 | all-reduce | flops 192 | bytes 1536 | tf_op jit(solution)/shard_map/psum | solution.py:31
  922.8 0.0 copy-done.3
  922.8 0.0 copy-done.4
  922.8 4.2 fusion.2
  927.0 1.1 fusion.35
  928.2 0.0 all-reduce.5.cloned.1.call-update
  928.2 0.0 all-reduce.7.cloned.1.call-start
  928.3 1.9 fusion.22
  930.1 0.0 all-reduce.7.cloned.1.call-update
  930.2 1.3 dynamic-slice
  932.1 107.7 %all-reduce.5.cloned.1.call-done = f32[160,128]{1,0:T(8,128)} async-done(((f32[160,128]{1,0:T(8,128)}), f32[160,128]{1,0:T(8,128)}) %all-reduce.5.cloned.1.call-update) | async-done | bytes 81936 | tf_op jit(solution)/shard_map/psum | solution.py:59
  1039.8 1.1 multiply_reduce_fusion.6
  1040.9 1.6 subtract_divide_fusion
  1042.5 291.0 %all-reduce.7.cloned.1.call-done = f32[128,4096]{1,0:T(8,128)} async-done(((f32[128,4096]{1,0:T(8,128)}), f32[128,4096]{1,0:T(8,128)}) %all-reduce.7.cloned.1.call-update) | async-done | bytes 2097168
  1333.5 1.0 multiply_reduce_fusion.7
  1334.5 276.8 %psum.70 = f32[4096]{0:T(1024)S(1)} all-reduce(f32[4096]{0:T(1024)S(1)} %multiply_reduce_fusion.7), channel_id=1, replica_groups=mesh['batch'=64,'proto'=16] {'batch'}, use_global_device_ids=true, to_apply=%region_19.20 | all-reduce | flops 4096 | bytes 32768 | tf_op jit(solution)/shard_map/psum | solution.py:70
  1611.3 1.6 subtract_divide_fusion.1
  (12 shorter events, 0.1 us)
Async XLA Ops:
  7.2 1032.6 %all-reduce.5.cloned.1.call-start = ((), (), s32[]{:S(2)}) async-start(), calls=%async_computation | async-start | bytes 163840 | tf_op jit(solution)/shard_map/psum | solution.py:59
  7.2 2.2 copy-start
  9.4 1.7 copy-start.2
  11.3 885.8 %copy-start.1 = (bf16[160,128]{1,0:T(8,128)(2,1)S(1)}, bf16[160,128]{1,0:T(8,128)(2,1)}, u32[]{:S(2)}) copy-start(bf16[160,128]{1,0:T(8,128)(2,1)} %param.5) | copy-start | bytes 122884
  896.9 25.9 %copy-start.3 = (s32[160]{0:T(256)S(1)}, s32[160]{0:T(256)}, u32[]{:S(2)}) copy-start(s32[160]{0:T(256)} %param.9) | copy-start | bytes 1924
  896.9 25.9 %copy-start.4 = (s32[160]{0:T(256)S(1)}, s32[160]{0:T(256)}, u32[]{:S(2)}) copy-start(s32[160]{0:T(256)} %param.8) | copy-start | bytes 1924
  928.2 405.3 %all-reduce.7.cloned.1.call-start = ((), (), s32[]{:S(2)}) async-start(), calls=%async_computation.1 | async-start | bytes 4194304
Sparse Core Ops, SparseCore 0:
  928.3 111.4 all-reduce.4
  1043.6 289.8 all-reduce.6
where the time goes:
time: 1620 us
  blocking collectives  1180 us (73%)
  waiting for transfers between devices  399 us (25%)
    psum x3, blocking collectives, per_device(): column = lax.psum(jnp.sum(scale_a[:, None] * expo, axis=0), 'batch')  840 us
    unnamed x3, waiting for transfers between devices  291 us
    psum x1, blocking collectives, per_device(): dots = lax.psum(jnp.sum(half_mine * dunit, axis=0), 'batch')  277 us
    psum x1, waiting for transfers between devices, per_device(): dz = lax.psum(dz_part, 'proto')  108 us
    psum x2, blocking collectives, per_device(): row_total = lax.psum(row_part, 'proto')  44.2 us
  transfers between devices with their start and end apart: 2, of which 2 were waited for; matrix products, arithmetic and copies ran while one was open for 0% of the time, Pallas kernels for 0%

commit v1 on v0

v1 whole, which is shorter than its diff:
```python
import functools

import jax
import jax.numpy as jnp
from jax import lax
from jax.experimental import pallas as pl
from jax.experimental.pallas import tpu as pltpu
from jax.sharding import Mesh
from jax.sharding import PartitionSpec as P

LOSS_SCALE = 16
EPS = 1e-06
TEACH_GAIN = 25.0
STUD_GAIN = 10.0
GRAD_GAIN = 160.0
BOT = 128
CB = 512
RC = 256
IMGS = 16
F32 = jnp.float32
BF16 = jnp.bfloat16
HI = lax.Precision.HIGHEST
VMEM_LIMIT = 56 * 1024 * 1024
INTERPRET = False


def mm(a, b, ca, cb, precision=None):
    return lax.dot_general(a, b, (((ca,), (cb,)), ((), ())), precision=precision, preferred_element_type=F32)


def call(kernel, out_shape, *args, scratch=(), flops=0):
    specs = pl.BlockSpec(memory_space=pltpu.VMEM)
    return pl.pallas_call(
        kernel,
        out_shape=out_shape,
        in_specs=[specs] * len(args),
        out_specs=jax.tree.map(lambda _: specs, out_shape),
        scratch_shapes=list(scratch),
        compiler_params=pltpu.CompilerParams(vmem_limit_bytes=VMEM_LIMIT),
        cost_estimate=pl.CostEstimate(flops=flops, bytes_accessed=0, transcendentals=0),
        interpret=INTERPRET,
    )(*args)


def row_unit(x):
    norm = jnp.sqrt(jnp.sum(x * x, axis=-1, keepdims=True) + EPS)
    return x / norm, norm


def selector(image, kind, teach_rows):
    shape = (teach_rows, image.shape[1])
    teach = lax.broadcasted_iota(jnp.int32, shape, 0)
    local = jnp.bitwise_and(jnp.broadcast_to(image, shape), IMGS - 1)
    kinds = jnp.broadcast_to(kind, shape)
    weight = jnp.where(kinds == 0, 0.5, jnp.where(jnp.bitwise_and(teach, 1) == 2 - kinds, 1.0, 0.0))
    return jnp.where(local == jnp.right_shift(teach, 1), weight, 0.0)


def spread(rows):
    parts = [jnp.broadcast_to(rows[i : i + 1, :], (128, 128)).T for i in range(rows.shape[0])]
    return jnp.concatenate(parts, axis=0)


def lane_sums(ref, n):
    parts = [jnp.sum(ref[i * 128 : (i + 1) * 128, :].T, axis=0, keepdims=True) for i in range(n)]
    return jnp.concatenate(parts, axis=0)


def peer_sum(ref, peers, size, start, rows):
    total = ref[start : start + rows, :]
    for p in range(1, peers):
        total = total + ref[p * size + start : p * size + start + rows, :]
    return total


def prep_kernel(student, teacher, image, kind, zp, sp):
    s_unit = row_unit(student[...].astype(F32))[0]
    t_unit = row_unit(teacher[...].astype(F32))[0]
    weights = selector(image[...], kind[...], teacher.shape[0])
    mixed = mm(weights.astype(BF16), s_unit.astype(BF16), 1, 0)
    core = lax.axis_index("c")
    th, sh = teacher.shape[0] // 2, student.shape[0] // 2
    first = core == 0
    zp[0:th, :] = jnp.where(first, t_unit[:th], t_unit[th:])
    zp[th : 2 * th, :] = jnp.where(first, mixed[:th], mixed[th:])
    sp[...] = jnp.where(first, s_unit[:sh], s_unit[sh:])


def unit_kernel(own, nx, proto, half, norm, mine):
    start = (lax.axis_index("z") * nx + lax.axis_index("x")) * own

    def step(j, carry):
        cols = pl.ds(pl.multiple_of(j * CB, CB), CB)
        v = proto[:, cols]
        n = jnp.sqrt(jnp.sum(v * v, axis=0, keepdims=True) + EPS)
        unit = v / n
        half[:, cols] = unit.astype(BF16)
        norm[:, cols] = n
        row = lax.broadcasted_iota(jnp.int32, unit.shape, 0)
        mine[:, cols] = jnp.concatenate(
            [jnp.sum(jnp.where(row == start + i, unit, 0.0), axis=0, keepdims=True) for i in range(own)], axis=0
        )
        return carry

    lax.fori_loop(0, proto.shape[1] // CB, step, 0)


def expo_block(t2, uh, gain, scr):
    u2 = jnp.concatenate([uh, uh], axis=0)
    col = jnp.zeros((8, uh.shape[1]), F32)
    for r in range(t2.shape[0] // RC):
        x = mm(t2[r * RC : (r + 1) * RC, :], u2, 1, 0)
        if gain is not None:
            g = gain[r * RC : (r + 1) * RC, :]
            x = x + jnp.concatenate([g] * (uh.shape[1] // 128), axis=1)
        e = jnp.exp(x)
        scr[r * RC : (r + 1) * RC, :] = e
        col = col + jnp.sum(e.reshape(RC // 8, 8, uh.shape[1]), axis=0)
    return jnp.sum(col, axis=0, keepdims=True)


def add_rows(scr, b, acc):
    for r in range(scr.shape[0] // RC):
        rows = slice(r * RC, (r + 1) * RC)
        e = scr[rows, :]
        total = acc[rows, :]
        for k in range(e.shape[1] // 128):
            lanes = slice(k * 128, (k + 1) * 128)
            total = total + e[:, lanes] * b[:, lanes]
        acc[rows, :] = total


def pass1_kernel(nz, groups, th, sh, g_ref, uh_ref, t2, s_half, mixed, pay, scr, acc, es_scr, s_acc):
    size = nz * 2 * th + sh
    for g in range(groups):
        for z in range(nz):
            src = g * size + z * 2 * th
            dst = (g * nz + z) * th
            t = g_ref[src : src + th, :].astype(BF16).astype(F32) * TEACH_GAIN
            hi = t.astype(BF16)
            t2[dst : dst + th, 0:BOT] = hi
            t2[dst : dst + th, BOT : 2 * BOT] = (t - hi.astype(F32)).astype(BF16)
            mixed[dst : dst + th, :] = g_ref[src + th : src + 2 * th, :]
        src = g * size + nz * 2 * th
        s_half[g * sh : (g + 1) * sh, :] = g_ref[src : src + sh, :].astype(BF16)
    acc[...] = jnp.zeros_like(acc)
    s_acc[...] = jnp.zeros_like(s_acc)
    n_t, n_s = t2.shape[0] // 128, s_half.shape[0] // 128
    top = n_t + (n_s + 7) // 8 * 8
    own = pl.multiple_of(lax.axis_index("x") * 2 * sh, 2 * sh)

    def step(j, e1):
        uh = uh_ref[:, pl.ds(pl.multiple_of(j * CB, CB), CB)]
        b = 1.0 / expo_block(t2, uh, None, scr)
        add_rows(scr, b, acc)
        for r in range(s_half.shape[0] // 128):
            rows = slice(r * 128, (r + 1) * 128)
            es = jnp.exp(mm(s_half[rows, :], uh, 1, 0) * STUD_GAIN)
            es_scr[rows, :] = es
            s_acc[rows, :] += sum(es[:, k * 128 : (k + 1) * 128] for k in range(CB // 128))
        return e1 + mm(es_scr[pl.ds(own, 2 * sh), :].astype(BF16), uh, 1, 1)

    e1 = lax.fori_loop(0, uh_ref.shape[1] // CB, step, jnp.zeros((2 * sh, BOT), F32))
    pay[0:n_t, :] = lane_sums(acc, n_t)
    pay[n_t:top, :] = jnp.zeros((top - n_t, 128), F32)
    pay[n_t : n_t + n_s, :] = lane_sums(s_acc, n_s)
    pay[top : top + 2 * sh, :] = e1


def student_kernel(nz, nx, own, peers, n_t, n_s, size, ag1, s_half, uh_ref, out, scale, a_scr):
    scale[...] = spread(GRAD_GAIN / peer_sum(ag1, peers, size, n_t, n_s))
    per = own + 1
    shape = (nz * per, BOT)
    row = lax.broadcasted_iota(jnp.int32, shape, 0)
    lane = lax.broadcasted_iota(jnp.int32, shape, 1)
    base = lax.axis_index("x") * own
    pick = jnp.zeros(shape, jnp.bool_)
    for z in range(nz):
        for i in range(own):
            pick = pick | ((row == z * per + i) & (lane == z * nx * own + base + i))
    picked = jnp.where(pick, 1.0, 0.0).astype(BF16)
    a_scr[...] = mm(picked, s_half[...], 1, 1).astype(BF16)
    n_c = uh_ref.shape[1] // 128

    def step(j, carry):
        uh = uh_ref[:, pl.ds(pl.multiple_of(j * CB, CB), CB)]
        d = jnp.zeros((nz * per, CB), F32)
        dots = jnp.zeros((8, CB), F32)
        for r in range(s_half.shape[0] // 128):
            rows = slice(r * 128, (r + 1) * 128)
            logits = mm(s_half[rows, :], uh, 1, 0)
            f = scale[rows, :]
            prob = jnp.exp(logits * STUD_GAIN) * jnp.concatenate([f] * (CB // 128), axis=1)
            dots = dots + jnp.sum((prob * logits).reshape(16, 8, CB), axis=0)
            d = d + mm(a_scr[:, rows], prob.astype(BF16), 1, 0)
        dot_row = jnp.sum(dots, axis=0, keepdims=True)
        for k in range(CB // 128):
            lanes = slice(k * 128, (k + 1) * 128)
            for z in range(nz):
                for i in range(own):
                    out[z, pl.ds(i * n_c + j * (CB // 128) + k, 1), :] = d[z * per + i : z * per + i + 1, lanes]
                out[z, pl.ds(own * n_c + j * (CB // 128) + k, 1), :] = dot_row[:, lanes]
        return carry

    lax.fori_loop(0, uh_ref.shape[1] // CB, step, 0)


def pass2_kernel(peers, size, n_t, ag, t2, uh_ref, pay, log_a, scr, acc, gain):
    la = -jnp.log(peer_sum(ag, peers, size, 0, n_t))
    log_a[...] = la
    gain[...] = spread(la)
    acc[...] = jnp.zeros_like(acc)

    def step(j, carry):
        uh = uh_ref[:, pl.ds(pl.multiple_of(j * CB, CB), CB)]
        b = 1.0 / expo_block(t2, uh, gain, scr)
        add_rows(scr, b, acc)
        return carry

    lax.fori_loop(0, uh_ref.shape[1] // CB, step, 0)
    pay[...] = lane_sums(acc, n_t)


def pass3_kernel(nz, th, peers, size, n_t, ag, log_a1, t2, uh_ref, pay, log_a2, b_out, scr, acc, gain):
    la = log_a1[...] - jnp.log(peer_sum(ag, peers, size, 0, n_t))
    log_a2[...] = la
    gain[...] = spread(la)
    acc[...] = jnp.zeros_like(acc)
    z, x = lax.axis_index("z"), lax.axis_index("x")
    starts = [pl.multiple_of(((2 * x + c) * nz + z) * th, th) for c in range(2)]

    def step(j, t_sum):
        cols = pl.ds(pl.multiple_of(j * CB, CB), CB)
        uh = uh_ref[:, cols]
        b = 1.0 / expo_block(t2, uh, gain, scr)
        b_out[:, cols] = b
        add_rows(scr, b, acc)
        mine = jnp.concatenate([scr[pl.ds(s, th), :] for s in starts], axis=0) * b
        return t_sum + mm(mine.astype(BF16), uh, 1, 1)

    t_sum = lax.fori_loop(0, uh_ref.shape[1] // CB, step, jnp.zeros((2 * th, BOT), F32))
    pay[0:n_t, :] = lane_sums(acc, n_t)
    pay[n_t:, :] = t_sum


def final_kernel(
    nz, nx, own, th, sh, peers, size1, n_s, size3, n_t,
    ag3, log_a2, b_ref, t2, uh_ref, mixed, d1, ag1, student, image, kind, norm, mine,
    gp, gs, gain, ma, s_scr, d_scr,
):
    x, z = lax.axis_index("x"), lax.axis_index("z")
    ratio = 1.0 / peer_sum(ag3, peers, size3, 0, n_t)
    gain[...] = spread(ratio)
    s_scr[...] = spread(1.0 / peer_sum(ag1, peers, size1, n_t, n_s))
    starts = [pl.multiple_of(((2 * x + c) * nz + z) * th, th) for c in range(2)]
    own_ratio = jnp.concatenate([gain[pl.ds(s, th), :] for s in starts], axis=0)
    t_sum = peer_sum(ag3, peers, size3, n_t, 2 * th) * own_ratio
    top = n_t + (n_s + 7) // 8 * 8
    e1 = peer_sum(ag1, peers, size1, top, 2 * sh) * s_scr[pl.ds(pl.multiple_of(x * 2 * sh, 2 * sh), 2 * sh), :]
    weights = selector(image[...], kind[...], 2 * th)
    dz = GRAD_GAIN * (e1 - mm(weights, t_sum, 0, 0, HI))
    s_unit, s_norm = row_unit(student[...].astype(F32))
    gs[...] = (dz - s_unit * jnp.sum(s_unit * dz, axis=1, keepdims=True)) / s_norm
    gain[...] = spread(jnp.exp(log_a2[...]) * ratio)
    for i in range(n_t):
        rows = slice(i * 128, (i + 1) * 128)
        ma[:, rows] = (mixed[rows, :] * gain[rows, :]).T.astype(BF16)
    total = d1[0]
    for k in range(1, nz):
        total = total + d1[k]
    d_scr[...] = total
    n_c = uh_ref.shape[1] // 128
    start = (z * nx + x) * own

    def step(j, carry):
        cols = pl.ds(pl.multiple_of(j * CB, CB), CB)
        uh = uh_ref[:, cols]
        u2 = jnp.concatenate([uh, uh], axis=0)
        d2 = jnp.zeros((BOT, CB), F32)
        for r in range(t2.shape[0] // RC):
            rows = slice(r * RC, (r + 1) * RC)
            e = jnp.exp(mm(t2[rows, :], u2, 1, 0)).astype(BF16)
            d2 = d2 + mm(ma[:, rows], e, 1, 0)
        d2 = d2 * (b_ref[:, cols] * GRAD_GAIN)
        dots2 = jnp.sum(uh.astype(F32) * d2, axis=0, keepdims=True)
        row = lax.broadcasted_iota(jnp.int32, d2.shape, 0)

        def early(i):
            return jnp.concatenate(
                [d_scr[pl.ds(i * n_c + j * (CB // 128) + k, 1), :] for k in range(CB // 128)], axis=1
            )

        dots = early(own) - dots2
        n = norm[:, cols]
        outs = []
        for i in range(own):
            late = jnp.sum(jnp.where(row == start + i, d2, 0.0), axis=0, keepdims=True)
            outs.append((early(i) - late - mine[i : i + 1, cols] * dots) / n)
        gp[:, cols] = jnp.concatenate(outs, axis=0)
        return carry

    lax.fori_loop(0, uh_ref.shape[1] // CB, step, 0)


def sds(shape, dtype=F32):
    return jax.ShapeDtypeStruct(shape, dtype)


def per_device(sizes, student_feat, teacher_feat, prototypes, crop_image, crop_kind):
    nz, nx, ny, nc = sizes
    peers = ny * nc
    groups = nx * nc
    crops, teach = student_feat.shape[0], teacher_feat.shape[0]
    th, sh = teach // 2, crops // 2
    cols = prototypes.shape[1]
    own = BOT // (nz * nx)
    teachers, gathered = teach * nz * nx, crops * nx
    n_t, n_s = teachers // 128, gathered // 128
    image, kind = crop_image.reshape(1, crops), crop_kind.reshape(1, crops)
    fl = 2 * teachers * cols * 256

    zp, sp = call(prep_kernel, (sds((2 * th, BOT)), sds((sh, BOT))), student_feat, teacher_feat, image, kind)
    got = lax.all_to_all(jnp.broadcast_to(zp[None], (nz, 2 * th, BOT)), "z", 0, 0, tiled=True)
    half, norm, mine = call(
        functools.partial(unit_kernel, own, nx), (sds((BOT, cols), BF16), sds((1, cols)), sds((own, cols))), prototypes
    )
    pack = jnp.concatenate([got.reshape(nz * 2 * th, BOT), sp], axis=0)
    everything = lax.all_gather(pack, ("x", "c"), tiled=True)

    big = [pltpu.VMEM((teachers, CB), F32), pltpu.VMEM((teachers, 128), F32)]
    size1 = n_t + (n_s + 7) // 8 * 8 + crops
    t2, s_half, mixed, pay1 = call(
        functools.partial(pass1_kernel, nz, groups, th, sh),
        (sds((teachers, 256), BF16), sds((gathered, BOT), BF16), sds((teachers, BOT)), sds((size1, 128))),
        everything,
        half,
        scratch=big + [pltpu.VMEM((gathered, CB), F32), pltpu.VMEM((gathered, 128), F32)],
        flops=fl,
    )
    ag1 = lax.all_gather(pay1, ("y", "c"), tiled=True)
    d1 = call(
        functools.partial(student_kernel, nz, nx, own, peers, n_t, n_s, size1),
        sds((nz, (own + 1) * cols // 128, 128)),
        ag1,
        s_half,
        half,
        scratch=[pltpu.VMEM((gathered, 128), F32), pltpu.VMEM((nz * (own + 1), gathered), BF16)],
        flops=fl // 4,
    )
    d1 = lax.all_to_all(d1, "z", 0, 0, tiled=True)
    pay2, log_a1 = call(
        functools.partial(pass2_kernel, peers, size1, n_t),
        (sds((n_t, 128)), sds((n_t, 128))),
        ag1,
        t2,
        half,
        scratch=big + [pltpu.VMEM((teachers, 128), F32)],
        flops=fl,
    )
    ag2 = lax.all_to_all(jnp.broadcast_to(pay2[None], (peers, n_t, 128)), ("y", "c"), 0, 0, tiled=True)
    pay3, log_a2, b3 = call(
        functools.partial(pass3_kernel, nz, th, peers, n_t, n_t),
        (sds((n_t + teach, 128)), sds((n_t, 128)), sds((1, cols))),
        ag2.reshape(peers * n_t, 128),
        log_a1,
        t2,
        half,
        scratch=big + [pltpu.VMEM((teachers, 128), F32)],
        flops=fl,
    )
    ag3 = lax.all_gather(pay3, ("y", "c"), tiled=True)
    grad_proto, grad_student = call(
        functools.partial(final_kernel, nz, nx, own, th, sh, peers, size1, n_s, n_t + teach, n_t),
        (sds((own, cols)), sds((crops, BOT))),
        ag3, log_a2, b3, t2, half, mixed, d1, ag1, student_feat, image, kind, norm, mine,
        scratch=[
            pltpu.VMEM((teachers, 128), F32),
            pltpu.VMEM((BOT, teachers), BF16),
            pltpu.VMEM((gathered, 128), F32),
            pltpu.VMEM(((own + 1) * cols // 128, 128), F32),
        ],
        flops=fl * 2,
    )
    return grad_proto, grad_student


def build(devices):
    grid = Mesh(devices, ("z", "x", "y", "c"))
    batch, proto = ("z", "x"), ("y", "c")
    return jax.shard_map(
        functools.partial(per_device, devices.shape),
        mesh=grid,
        in_specs=(P(batch, None), P(batch, None), P(None, proto), P(batch), P(batch)),
        out_specs=(P(batch, proto), P(batch, None)),
        check_vma=False,
    )


def solution(mesh):
    return build(mesh.devices.reshape(16, 4, 8, 2))
```

time: 1620 us -> 259 us (0.16)
  the two profiles are of different devices: /device:TPU:8 before, /device:TPU:1 now
where the time goes in v1:
time: 259 us; the launch traced here: 255 us
  Pallas kernels  85.1 us (33%)
  waiting for transfers between devices  81.7 us (32%)
  blocking collectives  52.5 us (20%)
  starting transfers between devices  17.6 us (7%)
  between operations  14.1 us (5%)
  local copies, waits for them, and re-layouts  2.97 us (1%)
    pallas_call x7, Pallas kernels, call(): pl.pallas_call(kernel, out_shape=out_shape, in_specs=[specs] * len(args),...  85.1 us
    all_gather x1, waiting for transfers between devices, per_device(): ag1 = lax.all_gather(pay1, ('y', 'c'), tiled=True)  47.7 us
    all_gather x1, waiting for transfers between devices, per_device(): everything = lax.all_gather(pack, ('x', 'c'), tiled=True)  33.6 us
    all_to_all x1, blocking collectives, per_device(): lax.all_to_all(jnp.broadcast_to(zp[None], (nz, 2 * th, BOT)), 'z', 0, 0,...  32.4 us
    all_gather x1, blocking collectives, per_device(): ag3 = lax.all_gather(pay3, ('y', 'c'), tiled=True)  20.2 us
    all_to_all x1, starting transfers between devices, per_device(): d1 = lax.all_to_all(d1, 'z', 0, 0, tiled=True)  12.8 us
  transfers between devices with their start and end apart: 4, of which 3 were waited for; matrix products, arithmetic and copies ran while one was open for 0% of the time, Pallas kernels for 12%

profile of v1, /device:TPU:1, one launch (start us, length us, event | category | flops | bytes accessed | tf_op | source)
XLA Modules:
  0.0 255.4 jit_solution(13662360743483974040)
XLA Ops:
  7.2 0.0 all-gather.3.cloned.1.call-start
  7.2 1.7 shard_map.68
  8.9 0.7 broadcast_in_dim.4
  9.6 32.4 %all_to_all.15 = f32[16,32,128]{2,1,0:T(8,128)S(1)} all-to-all(f32[16,32,128]{2,1,0:T(8,128)S(1)} %broadcast_in_dim.4), channel_id=1, replica_groups=mesh['z'=16,'x'=4,'y'=8,'c'=2] {'z'}, dimensions={0} | all-to-all | bytes 524288 | tf_op jit(solution)/shard_map/all_to_all | solution.py:323
  42.0 1.5 pad_maximum_fusion
  43.5 0.0 all-gather.3.cloned.1.call-update
  43.5 0.0 all-gather.5.cloned.1.call-start
  43.5 3.5 %shard_map.69 = (bf16[128,4096]{1,0:T(8,128)(2,1)}, f32[1,4096]{1,0:T(1,128)}, f32[2,4096]{1,0:T(2,128)}) custom-call(f32[128,4096]{1,0:T(8,128)} %proto.1), custom_call_target="tpu_custom_call" | custom-call | tf_op jit(solution)/shard_map/pallas_call | solution.py:33
  47.0 33.6 %all-gather.3.cloned.1.call-done.g_ref = f32[4736,128]{1,0:T(8,128)} async-done(((f32[592,128]{1,0:T(8,128)}), f32[4736,128]{1,0:T(8,128)}) %all-gather.3.cloned.1.call-update) | async-done | bytes 2424848 | tf_op jit(solution)/shard_map/all_gather | solution.py:328
  80.7 18.2 %shard_map.70 = (bf16[2048,256]{1,0:T(8,128)(2,1)}, bf16[640,128]{1,0:T(8,128)(2,1)}, f32[2048,128]{1,0:T(8,128)}, f32[184,128]{1,0:T(8,128)}) custom-call(f32[4736,128]{1,0:T(8,128)} %all-gather.3.cloned.1.call-done.g_ref, bf16[128,4096]{1,0:T(8,128)(2,1)} %get-tuple-element.18.uh_ref), custom_call_target="tpu_custom_call" | custom-call | flops 4294967296 | tf_op jit(solution)/shard_map/pallas_call | solution.py:33
  98.8 0.0 all-gather.5.cloned.1.call-update
  98.9 47.7 %all-gather.5.cloned.1.call-done.ag.ag1 = f32[2944,128]{1,0:T(8,128)} async-done(((f32[184,128]{1,0:T(8,128)}), f32[2944,128]{1,0:T(8,128)}) %all-gather.5.cloned.1.call-update) | async-done | bytes 1507344 | tf_op jit(solution)/shard_map/all_gather | solution.py:340
  146.6 13.9 %shard_map.71 = (f32[16,128]{1,0:T(8,128)}, f32[16,128]{1,0:T(8,128)}) custom-call(f32[2944,128]{1,0:T(8,128)} %all-gather.5.cloned.1.call-done.ag.ag1, bf16[2048,256]{1,0:T(8,128)(2,1)} %get-tuple-element.20.t2, bf16[128,4096]{1,0:T(8,128)(2,1)} %get-tuple-element.18.uh_ref), custom_call_target="tpu_custom_call" | custom-call | flops 4294967296 | tf_op jit(solution)/shard_map/pallas_call | solution.py:33
  160.4 1.4 broadcast_in_dim.5
  161.8 4.7 %all-to-all-start.1 = ((f32[16,16,128]{2,1,0:T(8,128)}), f32[16,16,128]{2,1,0:T(8,128)S(1)}, u32[]{:S(2)}, u32[]{:S(2)}) async-start(f32[16,16,128]{2,1,0:T(8,128)} %broadcast_in_dim.5), calls=%async_computation.1 | async-start | bytes 262144 | tf_op jit(solution)/shard_map/all_to_all | solution.py:360
  166.5 11.5 %shard_map.73 = f32[16,96,128]{2,1,0:T(8,128)} custom-call(f32[2944,128]{1,0:T(8,128)} %all-gather.5.cloned.1.call-done.ag.ag1, bf16[640,128]{1,0:T(8,128)(2,1)} %get-tuple-element.27.s_half, bf16[128,4096]{1,0:T(8,128)(2,1)} %get-tuple-element.18.uh_ref), custom_call_target="tpu_custom_call" | custom-call | flops 1073741824 | tf_op jit(solution)/shard_map/pallas_call | solution.py:33
  178.0 0.0 all-to-all-done.1
  178.0 0.0 copy-start.1
  178.0 12.8 %all-to-all-start.2 = ((f32[16,96,128]{2,1,0:T(8,128)}), f32[16,96,128]{2,1,0:T(8,128)S(1)}, u32[]{:S(2)}, u32[]{:S(2)}) async-start(f32[16,96,128]{2,1,0:T(8,128)} %shard_map.73), calls=%async_computation.2 | async-start | bytes 1572864 | tf_op jit(solution)/shard_map/all_to_all | solution.py:350
  190.8 0.0 copy-done.1
  190.8 15.7 %shard_map.72 = (f32[48,128]{1,0:T(8,128)}, f32[16,128]{1,0:T(8,128)}, f32[1,4096]{1,0:T(1,128)}) custom-call(f32[256,128]{1,0:T(8,128)} %bitcast.5, f32[16,128]{1,0:T(8,128)} %get-tuple-element.22.log_a1, bf16[2048,256]{1,0:T(8,128)(2,1)} %get-tuple-element.20.t2, bf16[128,4096]{1,0:T(8,128)(2,1)} %get-tuple-element.18.uh_ref), custom_call_target="tpu_custom_call" | custom-call | flops 4294967296 | tf_op jit(solution)/shard_map/pallas_call | solution.py:33
  206.4 20.2 %all_gather.11.ag3 = f32[768,128]{1,0:T(8,128)} all-gather(f32[48,128]{1,0:T(8,128)} %get-tuple-element.23), channel_id=1, replica_groups=mesh['z'=16,'x'=4,'y'=8,'c'=2] {'y','c'}, dimensions={0}, use_global_device_ids=true | all-gather | bytes 417792 | tf_op jit(solution)/shard_map/all_gather | solution.py:371
  226.6 0.3 all-to-all-done.2.d1
  226.9 0.0 copy-start
  226.9 0.9 copy-done
  227.7 20.8 %shard_map.74 = (f32[2,4096]{1,0:T(2,128)}, f32[160,128]{1,0:T(8,128)}) custom-call(f32[768,128]{1,0:T(8,128)} %all_gather.11.ag3, f32[16,128]{1,0:T(8,128)} %get-tuple-element.24.log_a2, f32[1,4096]{1,0:T(1,128)} %get-tuple-element.25.b_ref, bf16[2048,256]{1,0:T(8,128)(2,1)} %get-tuple-element.20.t2, bf16[128,4096]{1,0:T(8,128)(2,1)} %get-tuple-element.18.uh_ref, ...), custom_call_target="tpu_custom_call" | custom-call | flops 8589934592 | tf_op jit(solution)/shard_map/pallas_call | solution.py:33
Async XLA Ops:
  7.2 73.5 %all-gather.3.cloned.1.call-start = ((), (), s32[]{:S(2)}) async-start(), calls=%async_computation.3 | async-start | bytes 2727936 | tf_op jit(solution)/shard_map/all_gather | solution.py:328
  43.5 103.1 %all-gather.5.cloned.1.call-start = ((), (), s32[]{:S(2)}) async-start(), calls=%async_computation.4 | async-start | bytes 1601536 | tf_op jit(solution)/shard_map/all_gather | solution.py:340
  161.8 16.2 %all-to-all-start.1 = ((f32[16,16,128]{2,1,0:T(8,128)}), f32[16,16,128]{2,1,0:T(8,128)S(1)}, u32[]{:S(2)}, u32[]{:S(2)}) async-start(f32[16,16,128]{2,1,0:T(8,128)} %broadcast_in_dim.5), calls=%async_computation.1 | async-start | bytes 262144 | tf_op jit(solution)/shard_map/all_to_all | solution.py:360
  178.0 12.8 %copy-start.1 = (f32[16,16,128]{2,1,0:T(8,128)}, f32[16,16,128]{2,1,0:T(8,128)S(1)}, u32[]{:S(2)}) copy-start(f32[16,16,128]{2,1,0:T(8,128)S(1)} %all-to-all-done.1) | copy-start | bytes 393220
  178.0 48.9 %all-to-all-start.2 = ((f32[16,96,128]{2,1,0:T(8,128)}), f32[16,96,128]{2,1,0:T(8,128)S(1)}, u32[]{:S(2)}, u32[]{:S(2)}) async-start(f32[16,96,128]{2,1,0:T(8,128)} %shard_map.73), calls=%async_computation.2 | async-start | bytes 1572864 | tf_op jit(solution)/shard_map/all_to_all | solution.py:350
  226.9 0.9 copy-start
Sparse Core Ops, SparseCore 0:
  43.6 36.9 all-gather.2
  99.0 47.5 all-gather.4

commit v2 on v1

v2 whole, which is shorter than its diff:
```python
import functools

import jax
import jax.numpy as jnp
from jax import lax
from jax.experimental import pallas as pl
from jax.experimental.pallas import tpu as pltpu
from jax.sharding import Mesh
from jax.sharding import PartitionSpec as P

LOSS_SCALE = 16
EPS = 1e-06
LOG2E = 1.4426950408889634
TEACH_GAIN = 25.0 * LOG2E
STUD_GAIN = 10.0 * LOG2E
GRAD_GAIN = 160.0
BOT = 128
CB = 512
RC = 256
IMGS = 16
F32 = jnp.float32
BF16 = jnp.bfloat16
HI = lax.Precision.HIGHEST
VMEM_LIMIT = 28 * 1024 * 1024
INTERPRET = False


def mm(a, b, ca, cb, precision=None):
    return lax.dot_general(a, b, (((ca,), (cb,)), ((), ())), precision=precision, preferred_element_type=F32)


def call(kernel, out_shape, *args, scratch=(), flops=0, limit=VMEM_LIMIT):
    specs = pl.BlockSpec(memory_space=pltpu.VMEM)
    return pl.pallas_call(
        kernel,
        out_shape=out_shape,
        in_specs=[specs] * len(args),
        out_specs=jax.tree.map(lambda _: specs, out_shape),
        scratch_shapes=list(scratch),
        compiler_params=pltpu.CompilerParams(vmem_limit_bytes=limit),
        cost_estimate=pl.CostEstimate(flops=flops, bytes_accessed=0, transcendentals=0),
        interpret=INTERPRET,
    )(*args)


def row_unit(x):
    norm = jnp.sqrt(jnp.sum(x * x, axis=-1, keepdims=True) + EPS)
    return x / norm, norm


def selector(image, kind, teach_rows):
    shape = (teach_rows, image.shape[1])
    teach = lax.broadcasted_iota(jnp.int32, shape, 0)
    local = jnp.bitwise_and(jnp.broadcast_to(image, shape), IMGS - 1)
    kinds = jnp.broadcast_to(kind, shape)
    weight = jnp.where(kinds == 0, 0.5, jnp.where(jnp.bitwise_and(teach, 1) == 2 - kinds, 1.0, 0.0))
    return jnp.where(local == jnp.right_shift(teach, 1), weight, 0.0)


def spread(rows):
    parts = [jnp.broadcast_to(rows[i : i + 1, :], (128, 128)).T for i in range(rows.shape[0])]
    return jnp.concatenate(parts, axis=0)


def lane_sums(ref, n):
    parts = [jnp.sum(ref[i * 128 : (i + 1) * 128, :].T, axis=0, keepdims=True) for i in range(n)]
    return jnp.concatenate(parts, axis=0)


def prep_kernel(nz, student, teacher, image, kind, zp, sp):
    s_unit = row_unit(student[...].astype(F32))[0]
    t_unit = row_unit(teacher[...].astype(F32))[0]
    weights = selector(image[...], kind[...], teacher.shape[0])
    mixed = mm(weights.astype(BF16), s_unit.astype(BF16), 1, 0)
    th, sh = teacher.shape[0] // 2, student.shape[0] // 2
    first = lax.axis_index("c") == 0
    t = jnp.where(first, t_unit[:th], t_unit[th:])
    m = jnp.where(first, mixed[:th], mixed[th:])
    for p in range(nz):
        zp[p, 0:th, :] = t
        zp[p, th : 2 * th, :] = m
    sp[...] = jnp.where(first, s_unit[:sh], s_unit[sh:])


def unit_kernel(own, nx, proto, half, norm, mine):
    start = (lax.axis_index("z") * nx + lax.axis_index("x")) * own

    def step(j, carry):
        cols = pl.ds(pl.multiple_of(j * CB, CB), CB)
        v = proto[:, cols]
        n = jnp.sqrt(jnp.sum(v * v, axis=0, keepdims=True) + EPS)
        unit = v / n
        half[:, cols] = unit.astype(BF16)
        norm[:, cols] = n
        row = lax.broadcasted_iota(jnp.int32, unit.shape, 0)
        mine[:, cols] = jnp.concatenate(
            [jnp.sum(jnp.where(row == start + i, unit, 0.0), axis=0, keepdims=True) for i in range(own)], axis=0
        )
        return carry

    lax.fori_loop(0, proto.shape[1] // CB, step, 0)


def pack_kernel(nz, nx, got, sp, near, late):
    th = got.shape[1] // 2
    for p in range(nx):
        for z in range(nz):
            near[p, z * th : (z + 1) * th, :] = got[z, 0:th, :]
            late[p, z * th : (z + 1) * th, :] = got[z, th : 2 * th, :]
        near[p, nz * th :, :] = sp[...]


def powers(t2, u2, gain, r):
    x = mm(t2[r * RC : (r + 1) * RC, :], u2, 1, 0)
    if gain is not None:
        x = x + jnp.concatenate([gain[r * RC : (r + 1) * RC, :]] * (CB // 128), axis=1)
    return jnp.exp2(x)


def balance(t2, uh_ref, gain, scr, acc, first, finish, carry):
    n = uh_ref.shape[1] // CB
    acc[...] = jnp.zeros_like(acc)

    def block(j):
        return uh_ref[:, pl.ds(pl.multiple_of(j * CB, CB), CB)]

    def half(j, src, dst, b, carry):
        col = jnp.zeros((8, CB), F32)
        if dst is not None:
            uh = block(j)
            u2 = jnp.concatenate([uh, uh], axis=0)
        for r in range(t2.shape[0] // RC):
            rows = slice(r * RC, (r + 1) * RC)
            if dst is not None:
                e = powers(t2, u2, gain, r)
                scr[dst, rows, :] = e
                col = col + jnp.sum(e.reshape(RC // 8, 8, CB), axis=0)
            if src is not None:
                e = scr[src, rows, :]
                total = acc[rows, :]
                for k in range(CB // 128):
                    lanes = slice(k * 128, (k + 1) * 128)
                    total = total + e[:, lanes] * b[:, lanes]
                acc[rows, :] = total
        if src is not None and finish is not None:
            carry = finish(j - 1, b, scr.at[src], block(j - 1), carry)
        if dst is not None and first is not None:
            carry = first(uh, carry)
        return 1.0 / jnp.sum(col, axis=0, keepdims=True), carry

    b, carry = half(0, None, 0, None, carry)

    def step(i, state):
        b, carry = half(2 * i + 1, 0, 1, *state)
        return half(2 * i + 2, 1, 0, b, carry)

    b, carry = lax.fori_loop(0, n // 2 - 1, step, (b, carry))
    b, carry = half(n - 1, 0, 1, b, carry)
    return half(n, 1, None, b, carry)[1]


def pass1_kernel(nz, nx, peers, th, sh, near, other, uh_ref, t2, s_half, pay, scr, acc, es_scr, s_acc):
    rows_t = nz * th
    core = lax.axis_index("c")
    for g in range(2 * nx):
        both = jnp.where(core == g % 2, near[g // 2], other[g // 2])
        t = both[:rows_t].astype(BF16).astype(F32) * TEACH_GAIN
        hi = t.astype(BF16)
        t2[g * rows_t : (g + 1) * rows_t, 0:BOT] = hi
        t2[g * rows_t : (g + 1) * rows_t, BOT : 2 * BOT] = (t - hi.astype(F32)).astype(BF16)
        s_half[g * sh : (g + 1) * sh, :] = both[rows_t:].astype(BF16)
    s_acc[...] = jnp.zeros_like(s_acc)
    n_t, n_s = t2.shape[0] // 128, s_half.shape[0] // 128
    own = pl.multiple_of(lax.axis_index("x") * 2 * sh, 2 * sh)

    def first(uh, e1):
        for r in range(s_half.shape[0] // 128):
            rows = slice(r * 128, (r + 1) * 128)
            es = jnp.exp2(mm(s_half[rows, :], uh, 1, 0) * STUD_GAIN)
            es_scr[rows, :] = es
            s_acc[rows, :] += sum(es[:, k * 128 : (k + 1) * 128] for k in range(CB // 128))
        return e1 + mm(es_scr[pl.ds(own, 2 * sh), :].astype(BF16), uh, 1, 1)

    e1 = balance(t2, uh_ref, None, scr, acc, first, None, jnp.zeros((2 * sh, BOT), F32))
    sums = lane_sums(acc, n_t)
    totals = lane_sums(s_acc, n_s)
    part = 2 * sh // peers
    fill = jnp.zeros((16 - part - n_s, BOT), F32)
    for p in range(peers):
        pay[p, 0:n_t, :] = sums
        pay[p, n_t : n_t + 16, :] = jnp.concatenate([e1[p * part : (p + 1) * part, :], totals, fill], axis=0)


def total_of(ref, start, rows):
    total = ref[0, start : start + rows, :]
    for p in range(1, ref.shape[0]):
        total = total + ref[p, start : start + rows, :]
    return total


def student_kernel(nz, nx, own, n_t, n_s, ex1, s_half, uh_ref, late, out, token, scale, prob_scr):
    token[...] = jnp.zeros_like(token)
    scale[...] = spread(GRAD_GAIN / total_of(ex1, n_t, 16)[10 : 10 + n_s])
    shape = (nz * own, BOT)
    row = lax.broadcasted_iota(jnp.int32, shape, 0)
    lane = lax.broadcasted_iota(jnp.int32, shape, 1)
    base = lax.axis_index("x") * own
    pick = jnp.zeros(shape, jnp.bool_)
    for i in range(own):
        for z in range(nz):
            pick = pick | ((row == i * nz + z) & (lane == z * nx * own + base + i))
    picked = mm(jnp.where(pick, 1.0, 0.0).astype(BF16), s_half[...], 1, 1).astype(BF16)
    n_c = uh_ref.shape[1] // 128
    per = (own + 1) * n_c

    def step(j, carry):
        uh = uh_ref[:, pl.ds(pl.multiple_of(j * CB, CB), CB)]
        dots = jnp.zeros((8, CB), F32)
        for r in range(s_half.shape[0] // 128):
            rows = slice(r * 128, (r + 1) * 128)
            logits = mm(s_half[rows, :], uh, 1, 0)
            prob = jnp.exp2(logits * STUD_GAIN) * jnp.concatenate([scale[rows, :]] * (CB // 128), axis=1)
            dots = dots + jnp.sum((prob * logits).reshape(16, 8, CB), axis=0)
            prob_scr[rows, :] = prob.astype(BF16)
        d = mm(picked, prob_scr[...], 1, 0)
        dot_row = jnp.broadcast_to(jnp.sum(dots, axis=0, keepdims=True), (nz, CB))
        for k in range(CB // 128):
            lanes = slice(k * 128, (k + 1) * 128)
            at = j * (CB // 128) + k
            for i in range(own):
                out[pl.ds(i * n_c + at, nz, stride=per), :] = d[i * nz : (i + 1) * nz, lanes]
            out[pl.ds(own * n_c + at, nz, stride=per), :] = dot_row[:, lanes]
        return carry

    lax.fori_loop(0, uh_ref.shape[1] // CB, step, 0)


def pass2_kernel(n_t, ex1, t2, uh_ref, token, pay, log_a, scr, acc, gain):
    la = jnp.log(total_of(ex1, 0, n_t)) * -LOG2E
    log_a[...] = la
    gain[...] = spread(la)
    pay[n_t : n_t + 16, :] = total_of(ex1, n_t, 16)
    balance(t2, uh_ref, gain, scr, acc, None, None, 0)
    pay[0:n_t, :] = lane_sums(acc, n_t)


def own_rows(nz, th, g):
    z, x = lax.axis_index("z"), lax.axis_index("x")
    return [pl.multiple_of(((2 * x + c) * nz + z) * th, th) for c in range(g)]


def pass3_kernel(nz, th, n_t, ex2, log_a1, t2, uh_ref, pay, log_a2, b_out, scr, acc, gain):
    la = log_a1[...] - jnp.log(total_of(ex2, 0, n_t)) * LOG2E
    log_a2[...] = la
    gain[...] = spread(la)
    starts = own_rows(nz, th, 2)

    def finish(j, b, block, uh, t_sum):
        b_out[:, pl.ds(pl.multiple_of(j * CB, CB), CB)] = b
        mine = jnp.concatenate([block[pl.ds(s, th), :] for s in starts], axis=0) * b
        return t_sum + mm(mine.astype(BF16), uh, 1, 1)

    t_sum = balance(t2, uh_ref, gain, scr, acc, None, finish, jnp.zeros((2 * th, BOT), F32))
    pay[0:n_t, :] = lane_sums(acc, n_t)
    pay[n_t:, :] = t_sum


def final_kernel(
    nz, nx, own, th, sh, n_t, n_s,
    ex3, log_a2, b_ref, t2, uh_ref, late, other, d1, ex1, ex2, student, image, kind, norm, mine,
    gp, gs, gain, ma, s_scr, d_scr, scr,
):
    x, z = lax.axis_index("x"), lax.axis_index("z")
    peers = ex3.shape[0]
    ratio = 1.0 / total_of(ex3, 0, n_t)
    gain[...] = spread(ratio)
    s_scr[...] = spread(1.0 / total_of(ex1, n_t, 16)[10 : 10 + n_s])
    own_ratio = jnp.concatenate([gain[pl.ds(s, th), :] for s in own_rows(nz, th, 2)], axis=0)
    t_sum = total_of(ex3, n_t, 2 * th) * own_ratio
    part = 2 * sh // peers
    e1 = jnp.concatenate([ex2[p, n_t : n_t + part, :] for p in range(peers)], axis=0)
    e1 = e1 * s_scr[pl.ds(pl.multiple_of(x * 2 * sh, 2 * sh), 2 * sh), :]
    weights = selector(image[...], kind[...], 2 * th)
    dz = GRAD_GAIN * (e1 - mm(weights, t_sum, 0, 0, HI))
    s_unit, s_norm = row_unit(student[...].astype(F32))
    gs[...] = (dz - s_unit * jnp.sum(s_unit * dz, axis=1, keepdims=True)) / s_norm
    gain[...] = spread(jnp.exp2(log_a2[...]) * ratio)
    half_rows = late.shape[1]
    core = lax.axis_index("c")
    for i in range(n_t):
        g, q = (i * 128) // half_rows, (i * 128) % half_rows
        mixed = jnp.where(core == g % 2, late[g // 2, q : q + 128, :], other[g // 2, q : q + 128, :])
        ma[:, i * 128 : (i + 1) * 128] = (mixed * gain[i * 128 : (i + 1) * 128, :]).T.astype(BF16)
    total = d1[0]
    for k in range(1, nz):
        total = total + d1[k]
    d_scr[...] = total
    n_c = uh_ref.shape[1] // 128
    start = (z * nx + x) * own
    n = uh_ref.shape[1] // CB

    def fill(j, dst):
        uh = uh_ref[:, pl.ds(pl.multiple_of(j * CB, CB), CB)]
        u2 = jnp.concatenate([uh, uh], axis=0)
        for r in range(t2.shape[0] // RC):
            scr[dst, r * RC : (r + 1) * RC, :] = powers(t2, u2, None, r).astype(BF16)

    def use(j, src):
        cols = pl.ds(pl.multiple_of(j * CB, CB), CB)
        d2 = mm(ma[...], scr[src], 1, 0) * (b_ref[:, cols] * GRAD_GAIN)
        dots2 = jnp.sum(uh_ref[:, cols].astype(F32) * d2, axis=0, keepdims=True)
        row = lax.broadcasted_iota(jnp.int32, d2.shape, 0)

        def early(i):
            return jnp.concatenate(
                [d_scr[pl.ds(i * n_c + j * (CB // 128) + k, 1), :] for k in range(CB // 128)], axis=1
            )

        dots = early(own) - dots2
        outs = []
        for i in range(own):
            late = jnp.sum(jnp.where(row == start + i, d2, 0.0), axis=0, keepdims=True)
            outs.append((early(i) - late - mine[i : i + 1, cols] * dots) / norm[:, cols])
        gp[:, cols] = jnp.concatenate(outs, axis=0)

    fill(0, 0)

    def step(i, carry):
        fill(2 * i + 1, 1)
        use(2 * i, 0)
        fill(2 * i + 2, 0)
        use(2 * i + 1, 1)
        return carry

    lax.fori_loop(0, n // 2 - 1, step, 0)
    fill(n - 1, 1)
    use(n - 2, 0)
    use(n - 1, 1)


def sds(shape, dtype=F32):
    return jax.ShapeDtypeStruct(shape, dtype)


def swap(x, axes):
    return lax.all_to_all(x, axes, 0, 0, tiled=True)


def per_device(sizes, student_feat, teacher_feat, prototypes, crop_image, crop_kind):
    nz, nx, ny, nc = sizes
    peers = ny * nc
    crops, teach = student_feat.shape[0], teacher_feat.shape[0]
    th, sh = teach // 2, crops // 2
    cols = prototypes.shape[1]
    own = BOT // (nz * nx)
    teachers, gathered = teach * nz * nx, crops * nx
    n_t, n_s = teachers // 128, gathered // 128
    image, kind = crop_image.reshape(1, crops), crop_kind.reshape(1, crops)
    fl = 2 * teachers * cols * 256

    zp, sp = call(
        functools.partial(prep_kernel, nz),
        (sds((nz, 2 * th, BOT)), sds((sh, BOT))),
        student_feat,
        teacher_feat,
        image,
        kind,
        limit=58 * 1024 * 1024,
    )
    half, norm, mine = call(
        functools.partial(unit_kernel, own, nx),
        (sds((BOT, cols), BF16), sds((1, cols)), sds((own, cols))),
        prototypes,
        flops=fl // 2,
    )
    got = swap(zp, "z")
    near, late = call(
        functools.partial(pack_kernel, nz, nx),
        (sds((nx, nz * th + sh, BOT)), sds((nx, nz * th, BOT))),
        got,
        sp,
    )
    near = swap(near, "x")
    near_other = lax.ppermute(near, "c", [(0, 1), (1, 0)])
    late = swap(late, "x")
    late_other = lax.ppermute(late, "c", [(0, 1), (1, 0)])

    big = [pltpu.VMEM((2, teachers, CB), F32), pltpu.VMEM((teachers, 128), F32)]
    t2, s_half, pay1 = call(
        functools.partial(pass1_kernel, nz, nx, peers, th, sh),
        (sds((teachers, 256), BF16), sds((gathered, BOT), BF16), sds((peers, n_t + 16, 128))),
        near,
        near_other,
        half,
        scratch=big + [pltpu.VMEM((gathered, CB), F32), pltpu.VMEM((gathered, 128), F32)],
        flops=fl,
    )
    ex1 = swap(pay1, ("y", "c"))
    d1, token = call(
        functools.partial(student_kernel, nz, nx, own, n_t, n_s),
        (sds((nz * (own + 1) * cols // 128, 128)), sds((8, 128))),
        ex1,
        s_half,
        half,
        late,
        scratch=[pltpu.VMEM((gathered, 128), F32), pltpu.VMEM((gathered, CB), BF16)],
        flops=fl // 2,
    )
    d1 = swap(d1.reshape(nz, (own + 1) * cols // 128, 128), "z")
    pay2, log_a1 = call(
        functools.partial(pass2_kernel, n_t),
        (sds((n_t + 16, 128)), sds((n_t, 128))),
        ex1,
        t2,
        half,
        token,
        scratch=big + [pltpu.VMEM((teachers, 128), F32)],
        flops=fl // 4,
    )
    ex2 = lax.all_gather(pay2, ("y", "c"))
    pay3, log_a2, b3 = call(
        functools.partial(pass3_kernel, nz, th, n_t),
        (sds((n_t + teach, 128)), sds((n_t, 128)), sds((1, cols))),
        ex2,
        log_a1,
        t2,
        half,
        scratch=big + [pltpu.VMEM((teachers, 128), F32)],
        flops=fl // 4,
    )
    ex3 = lax.all_gather(pay3, ("y", "c"))
    return call(
        functools.partial(final_kernel, nz, nx, own, th, sh, n_t, n_s),
        (sds((own, cols)), sds((crops, BOT))),
        ex3, log_a2, b3, t2, half, late, late_other, d1, ex1, ex2, student_feat, image, kind, norm, mine,
        scratch=[
            pltpu.VMEM((teachers, 128), F32),
            pltpu.VMEM((BOT, teachers), BF16),
            pltpu.VMEM((gathered, 128), F32),
            pltpu.VMEM(((own + 1) * cols // 128, 128), F32),
            pltpu.VMEM((2, teachers, CB), BF16),
        ],
        flops=fl * 2,
    )


def build(devices):
    grid = Mesh(devices, ("z", "x", "y", "c"))
    batch, proto = ("z", "x"), ("y", "c")
    return jax.shard_map(
        functools.partial(per_device, devices.shape),
        mesh=grid,
        in_specs=(P(batch, None), P(batch, None), P(None, proto), P(batch), P(batch)),
        out_specs=(P(batch, proto), P(batch, None)),
        check_vma=False,
    )


def solution(mesh):
    return build(mesh.devices.reshape(16, 4, 8, 2))
```

time: 259 us -> 172 us (0.66); the launches traced: 255 us -> 172 us
  waiting for transfers between devices: 81.7 us -> 0.01 us
  blocking collectives: 52.5 us -> 95.5 us
  Pallas kernels: 85.1 us -> 44.4 us
  between operations: 14.1 us -> 0.77 us
  local copies, waits for them, and re-layouts: 2.97 us -> 8.25 us
  starting transfers between devices: 17.6 us -> 22.6 us
    all_gather x2 -> x0, waiting for transfers between devices: 81.4 us -> none  [the longest x1 47.7 us: per_device(): ag1 = lax.all_gather(pay1, ('y', 'c'), tiled=True)]
    pallas_call x7 -> x8, Pallas kernels: 85.1 us -> 44.4 us  [call(): pl.pallas_call(kernel, out_shape=out_shape, in_specs=[specs] * len(args),...]
    all_to_all x1 -> x3, blocking collectives: 32.4 us -> 62.9 us  [swap(): return lax.all_to_all(x, axes, 0, 0, tiled=True)]
    all_gather x1 -> x2, blocking collectives: 20.2 us -> 32.6 us  [the longest x1 17.2 us: per_device(): ex3 = lax.all_gather(pay3, ('y', 'c'))]
    ppermute x0 -> x2, starting transfers between devices: none -> 11.4 us  [the longest x1 9.51 us: per_device(): near_other = lax.ppermute(near, 'c', [(0, 1), (1, 0)])]
    unnamed x4 -> x22, local copies, waits for them, and re-layouts: 0.88 us -> 8.25 us
    all_to_all x2, starting transfers between devices: 17.5 us -> 11.2 us  [swap(): return lax.all_to_all(x, axes, 0, 0, tiled=True)]
  transfers between devices with their start and end apart: 4 -> 4, of which waited for: 3 -> 0; matrix products, arithmetic and copies ran while one was open for 0% -> 0% of each run, Pallas kernels for 12% -> 16%
where the time goes in v2:
time: 172 us
  blocking collectives  95.5 us (56%)
  Pallas kernels  44.4 us (26%)
  starting transfers between devices  22.6 us (13%)
  local copies, waits for them, and re-layouts  8.25 us (5%)
    all_to_all x3, blocking collectives, swap(): return lax.all_to_all(x, axes, 0, 0, tiled=True)  62.9 us
    pallas_call x8, Pallas kernels, call(): pl.pallas_call(kernel, out_shape=out_shape, in_specs=[specs] * len(args),...  44.4 us
    all_gather x1, blocking collectives, per_device(): ex3 = lax.all_gather(pay3, ('y', 'c'))  17.2 us
    all_gather x1, blocking collectives, per_device(): ex2 = lax.all_gather(pay2, ('y', 'c'))  15.4 us
    all_to_all x2, starting transfers between devices, swap(): return lax.all_to_all(x, axes, 0, 0, tiled=True)  11.2 us
    ppermute x1, starting transfers between devices, per_device(): near_other = lax.ppermute(near, 'c', [(0, 1), (1, 0)])  9.51 us
    unnamed x22, local copies, waits for them, and re-layouts  8.25 us
  transfers between devices with their start and end apart: 4, of which 0 were waited for; matrix products, arithmetic and copies ran while one was open for 0% of the time, Pallas kernels for 16%

profile of v2, /device:TPU:1, one launch (start us, length us, event | category | flops | bytes accessed | tf_op | source)
XLA Modules:
  0.0 171.5 jit_solution(12674599553874533706)
XLA Ops:
  0.6 1.8 %shard_map.68 = (f32[16,32,128]{2,1,0:T(8,128)}, f32[80,128]{1,0:T(8,128)}) custom-call(bf16[160,128]{1,0:T(8,128)(2,1)} %student.3, bf16[32,128]{1,0:T(8,128)(2,1)} %teacher.1, s32[1,160]{1,0:T(1,128)} %bitcast.8, s32[1,160]{1,0:T(1,128)} %bitcast.10), custom_call_target="tpu_custom_call" | custom-call | tf_op jit(solution)/shard_map/pallas_call | solution.py:34
  2.4 32.5 %all_to_all.25.got = f32[16,32,128]{2,1,0:T(8,128)S(1)} all-to-all(f32[16,32,128]{2,1,0:T(8,128)} %get-tuple-element.19), channel_id=1, replica_groups=mesh['z'=16,'x'=4,'y'=8,'c'=2] {'z'}, dimensions={0} | all-to-all | bytes 524288 | tf_op jit(solution)/shard_map/all_to_all | solution.py:346
  34.9 0.0 copy-start
  34.9 0.8 copy-done
  35.7 0.9 shard_map.69
  36.6 11.6 %all_to_all.26.near = f32[4,336,128]{2,1,0:T(8,128)S(1)} all-to-all(f32[4,336,128]{2,1,0:T(8,128)S(1)} %get-tuple-element.21), channel_id=1, replica_groups=mesh['z'=16,'x'=4,'y'=8,'c'=2] {'x'}, dimensions={0} | all-to-all | bytes 1376256 | tf_op jit(solution)/shard_map/all_to_all | solution.py:346
  48.2 9.5 %collective-permute-start = (f32[4,336,128]{2,1,0:T(8,128)S(1)}, f32[4,336,128]{2,1,0:T(8,128)S(1)}, u32[]{:S(2)}, u32[]{:S(2)}) collective-permute-start(f32[4,336,128]{2,1,0:T(8,128)S(1)} %all_to_all.26.near), channel_id=1, source_target_pairs={{0,1},{1,0},{2,3},{3,2},{4,5},{5,4},{6,7},{7,6},{8,9},{9,8},{10,11... | collective-permute-start | bytes 2064392 | tf_op jit(solution)/shard_map/ppermute | solution.py:384
  57.7 0.0 copy-start.4
  57.7 1.6 copy-done.4
  59.3 0.9 shard_map.70
  60.2 0.0 copy-start.5
  60.3 3.5 %all-to-all-start.3 = ((f32[4,256,128]{2,1,0:T(8,128)}), f32[4,256,128]{2,1,0:T(8,128)S(1)}, u32[]{:S(2)}, u32[]{:S(2)}) async-start(f32[4,256,128]{2,1,0:T(8,128)} %get-tuple-element.26), calls=%async_computation.3 | async-start | bytes 1048576 | tf_op jit(solution)/shard_map/all_to_all | solution.py:346
  63.7 0.0 collective-permute-done.other
  63.8 9.6 %shard_map.71 = (bf16[2048,256]{1,0:T(8,128)(2,1)S(1)}, bf16[640,128]{1,0:T(8,128)(2,1)S(1)}, f32[16,32,128]{2,1,0:T(8,128)S(1)}) custom-call(f32[4,336,128]{2,1,0:T(8,128)S(1)} %all_to_all.26.near, f32[4,336,128]{2,1,0:T(8,128)S(1)} %collective-permute-done.other, bf16[128,4096]{1,0:T(8,128)(2,1)S(1)} %get-tuple-element.22.uh_ref), custom_call_target="tpu_custom_call" | custom-call | flops 4294967296 | tf_op jit(solution)/shard_map/pallas_call | solution.py:34
  73.3 0.0 copy-start.8
  73.3 1.0 copy-done.8
  74.3 0.0 all-to-all-done.3.late
  74.3 18.7 %all_to_all.27.ex1 = f32[16,32,128]{2,1,0:T(8,128)S(1)} all-to-all(f32[16,32,128]{2,1,0:T(8,128)S(1)} %get-tuple-element.23), channel_id=1, replica_groups=mesh['z'=16,'x'=4,'y'=8,'c'=2] {'y','c'}, dimensions={0} | all-to-all | bytes 524288 | tf_op jit(solution)/shard_map/all_to_all | solution.py:346
  93.0 0.0 copy-done.5
  93.0 5.7 %shard_map.72 = (f32[1536,128]{1,0:T(8,128)}, f32[8,128]{1,0:T(8,128)S(1)}) custom-call(f32[16,32,128]{2,1,0:T(8,128)S(1)} %all_to_all.27.ex1, bf16[640,128]{1,0:T(8,128)(2,1)S(1)} %get-tuple-element.25.s_half, bf16[128,4096]{1,0:T(8,128)(2,1)S(1)} %get-tuple-element.22.uh_ref, f32[4,256,128]{2,1,0:T(8,128)S(1)} %all-to-all-done.3.late), custom_call_target="tpu_custom_call" | custom-call | flops 2147483648 | tf_op jit(solution)/shard_map/pallas_call | solution.py:34
  98.8 7.7 %all-to-all-start.4 = ((f32[16,96,128]{2,1,0:T(8,128)}), f32[16,96,128]{2,1,0:T(8,128)S(1)}, u32[]{:S(2)}, u32[]{:S(2)}) async-start(f32[16,96,128]{2,1,0:T(8,128)} %bitcast.4), calls=%async_computation.4 | async-start | bytes 1572864 | tf_op jit(solution)/shard_map/all_to_all | solution.py:346
  106.5 1.9 %collective-permute-start.1 = (f32[4,256,128]{2,1,0:T(8,128)S(1)}, f32[4,256,128]{2,1,0:T(8,128)S(1)}, u32[]{:S(2)}, u32[]{:S(2)}) collective-permute-start(f32[4,256,128]{2,1,0:T(8,128)S(1)} %all-to-all-done.3.late), channel_id=1, source_target_pairs={{0,1},{1,0},{2,3},{3,2},{4,5},{5,4},{6,7},{7,6},{8,9},{9,8},{10,11... | collective-permute-start | bytes 1572872 | tf_op jit(solution)/shard_map/ppermute | solution.py:386
  108.4 0.0 copy-start.6
  108.4 1.2 copy-done.6
  109.6 0.0 copy-start.9
  109.6 1.2 copy-done.9
  110.9 7.4 %shard_map.73 = (f32[32,128]{1,0:T(8,128)S(1)}, f32[16,128]{1,0:T(8,128)S(1)}) custom-call(f32[16,32,128]{2,1,0:T(8,128)S(1)} %all_to_all.27.ex1, bf16[2048,256]{1,0:T(8,128)(2,1)S(1)} %copy-done.9, bf16[128,4096]{1,0:T(8,128)(2,1)S(1)} %copy-done.6, f32[8,128]{1,0:T(8,128)S(1)} %get-tuple-element.27.token), custom_call_target="tpu_custom_call" | custom-call | flops 1073741824 | tf_op jit(solution)/shard_map/pallas_call | solution.py:34
  118.2 15.4 %all-gather = f32[512,128]{1,0:T(8,128)S(1)} all-gather(f32[32,128]{1,0:T(8,128)S(1)} %get-tuple-element.28), channel_id=2, replica_groups=mesh['z'=16,'x'=4,'y'=8,'c'=2] {'y','c'}, dimensions={0}, use_global_device_ids=true | all-gather | bytes 278528 | tf_op jit(solution)/shard_map/all_gather | solution.py:420
  133.6 0.0 copy-start.1
  133.6 0.0 copy-start.2
  133.6 0.0 copy-start.3
  133.6 9.3 %shard_map.74 = (f32[48,128]{1,0:T(8,128)S(1)}, f32[16,128]{1,0:T(8,128)S(1)}, f32[1,4096]{1,0:T(1,128)S(1)}) custom-call(f32[16,32,128]{2,1,0:T(8,128)S(1)} %bitcast.6, f32[16,128]{1,0:T(8,128)S(1)} %get-tuple-element.29.log_a1, bf16[2048,256]{1,0:T(8,128)(2,1)S(1)} %copy-done.9, bf16[128,4096]{1,0:T(8,128)(2,1)S(1)} %copy-done.6), custom_call_target="tpu_custom_call" | custom-call | flops 1073741824 | tf_op jit(solution)/shard_map/pallas_call | solution.py:34
  142.9 17.2 %all-gather.1 = f32[768,128]{1,0:T(8,128)S(1)} all-gather(f32[48,128]{1,0:T(8,128)S(1)} %get-tuple-element.30), channel_id=3, replica_groups=mesh['z'=16,'x'=4,'y'=8,'c'=2] {'y','c'}, dimensions={0}, use_global_device_ids=true | all-gather | bytes 417792 | tf_op jit(solution)/shard_map/all_gather | solution.py:431
  160.0 0.0 collective-permute-done.1.other
  160.0 0.0 all-to-all-done.4.d1
  160.1 0.0 copy-done.1
  160.1 0.0 copy-done.2
  160.1 0.0 copy-done.3
  160.1 0.0 copy-start.7
  160.1 1.2 copy-done.7
  161.3 0.0 copy-start.10
  161.3 1.2 copy-done.10
  162.5 9.0 %shard_map.75 = (f32[2,4096]{1,0:T(2,128)}, f32[160,128]{1,0:T(8,128)}) custom-call(f32[16,48,128]{2,1,0:T(8,128)S(1)} %bitcast.5, f32[16,128]{1,0:T(8,128)S(1)} %get-tuple-element.31.log_a2, f32[1,4096]{1,0:T(1,128)S(1)} %get-tuple-element.32.b_ref, bf16[2048,256]{1,0:T(8,128)(2,1)S(1)} %copy-done.10, bf16[128,4096]{1,0:T(8,128)(2,1)S(1)} %copy-done.7, ...), custom_call_target="tpu_custom_call" | custom-call | flops 8589934592 | tf_op jit(solution)/shard_map/pallas_call | solution.py:34
Async XLA Ops:
  34.9 0.8 copy-start
  48.2 15.6 %collective-permute-start = (f32[4,336,128]{2,1,0:T(8,128)S(1)}, f32[4,336,128]{2,1,0:T(8,128)S(1)}, u32[]{:S(2)}, u32[]{:S(2)}) collective-permute-start(f32[4,336,128]{2,1,0:T(8,128)S(1)} %all_to_all.26.near), channel_id=1, source_target_pairs={{0,1},{1,0},{2,3},{3,2},{4,5},{5,4},{6,7},{7,6},{8,9},{9,8},{10,11... | collective-permute-start | bytes 2064392 | tf_op jit(solution)/shard_map/ppermute | solution.py:384
  57.7 1.6 copy-start.4
  60.2 32.8 %copy-start.5 = (bf16[128,4096]{1,0:T(8,128)(2,1)}, bf16[128,4096]{1,0:T(8,128)(2,1)S(1)}, u32[]{:S(2)}) copy-start(bf16[128,4096]{1,0:T(8,128)(2,1)S(1)} %get-tuple-element.22.uh_ref) | copy-start | bytes 3145732
  60.3 14.1 %all-to-all-start.3 = ((f32[4,256,128]{2,1,0:T(8,128)}), f32[4,256,128]{2,1,0:T(8,128)S(1)}, u32[]{:S(2)}, u32[]{:S(2)}) async-start(f32[4,256,128]{2,1,0:T(8,128)} %get-tuple-element.26), calls=%async_computation.3 | async-start | bytes 1048576 | tf_op jit(solution)/shard_map/all_to_all | solution.py:346
  73.3 1.0 copy-start.8
  98.8 61.3 %all-to-all-start.4 = ((f32[16,96,128]{2,1,0:T(8,128)}), f32[16,96,128]{2,1,0:T(8,128)S(1)}, u32[]{:S(2)}, u32[]{:S(2)}) async-start(f32[16,96,128]{2,1,0:T(8,128)} %bitcast.4), calls=%async_computation.4 | async-start | bytes 1572864 | tf_op jit(solution)/shard_map/all_to_all | solution.py:346
  106.5 53.6 %collective-permute-start.1 = (f32[4,256,128]{2,1,0:T(8,128)S(1)}, f32[4,256,128]{2,1,0:T(8,128)S(1)}, u32[]{:S(2)}, u32[]{:S(2)}) collective-permute-start(f32[4,256,128]{2,1,0:T(8,128)S(1)} %all-to-all-done.3.late), channel_id=1, source_target_pairs={{0,1},{1,0},{2,3},{3,2},{4,5},{5,4},{6,7},{7,6},{8,9},{9,8},{10,11... | collective-permute-start | bytes 1572872 | tf_op jit(solution)/shard_map/ppermute | solution.py:386
  108.4 1.2 copy-start.6
  109.6 1.2 copy-start.9
  133.6 26.5 %copy-start.1 = (bf16[160,128]{1,0:T(8,128)(2,1)S(1)}, bf16[160,128]{1,0:T(8,128)(2,1)}, u32[]{:S(2)}) copy-start(bf16[160,128]{1,0:T(8,128)(2,1)} %student.3) | copy-start | bytes 122884
  133.6 26.5 %copy-start.2 = (s32[160]{0:T(256)S(1)}, s32[160]{0:T(256)}, u32[]{:S(2)}) copy-start(s32[160]{0:T(256)} %param.8) | copy-start | bytes 1924
  133.6 26.5 %copy-start.3 = (s32[160]{0:T(256)S(1)}, s32[160]{0:T(256)}, u32[]{:S(2)}) copy-start(s32[160]{0:T(256)} %param.9) | copy-start | bytes 1924
  160.1 1.2 copy-start.7
  161.3 1.2 copy-start.10

commit v3 on v2

--- a/solution.py
+++ b/solution.py
@@ -21,7 +21,7 @@
 F32 = jnp.float32
 BF16 = jnp.bfloat16
 HI = lax.Precision.HIGHEST
-VMEM_LIMIT = 28 * 1024 * 1024
+VMEM_LIMIT = 16 * 1024 * 1024
 INTERPRET = False
 
 
@@ -67,19 +67,18 @@
     return jnp.concatenate(parts, axis=0)
 
 
-def prep_kernel(nz, student, teacher, image, kind, zp, sp):
+def prep_kernel(nz, student, teacher, image, kind, zp):
     s_unit = row_unit(student[...].astype(F32))[0]
     t_unit = row_unit(teacher[...].astype(F32))[0]
     weights = selector(image[...], kind[...], teacher.shape[0])
     mixed = mm(weights.astype(BF16), s_unit.astype(BF16), 1, 0)
-    th, sh = teacher.shape[0] // 2, student.shape[0] // 2
+    th = teacher.shape[0] // 2
     first = lax.axis_index("c") == 0
     t = jnp.where(first, t_unit[:th], t_unit[th:])
     m = jnp.where(first, mixed[:th], mixed[th:])
     for p in range(nz):
         zp[p, 0:th, :] = t
         zp[p, th : 2 * th, :] = m
-    sp[...] = jnp.where(first, s_unit[:sh], s_unit[sh:])
 
 
 def unit_kernel(own, nx, proto, half, norm, mine):
@@ -101,13 +100,15 @@
     lax.fori_loop(0, proto.shape[1] // CB, step, 0)
 
 
-def pack_kernel(nz, nx, got, sp, near, late):
-    th = got.shape[1] // 2
+def pack_kernel(nz, nx, got, student, near, late):
+    th, sh = got.shape[1] // 2, student.shape[0] // 2
+    s_unit = row_unit(student[...].astype(F32))[0]
+    sp = jnp.where(lax.axis_index("c") == 0, s_unit[:sh], s_unit[sh:])
     for p in range(nx):
         for z in range(nz):
             near[p, z * th : (z + 1) * th, :] = got[z, 0:th, :]
             late[p, z * th : (z + 1) * th, :] = got[z, th : 2 * th, :]
-        near[p, nz * th :, :] = sp[...]
+        near[p, nz * th :, :] = sp
 
 
 def powers(t2, u2, gain, r):
@@ -198,7 +199,7 @@
     return total
 
 
-def student_kernel(nz, nx, own, n_t, n_s, ex1, s_half, uh_ref, late, out, token, scale, prob_scr):
+def student_kernel(nz, nx, own, n_t, n_s, ex1, s_half, uh_ref, late, log_a1, out, token, scale, prob_scr):
     token[...] = jnp.zeros_like(token)
     scale[...] = spread(GRAD_GAIN / total_of(ex1, n_t, 16)[10 : 10 + n_s])
     shape = (nz * own, BOT)
@@ -235,13 +236,16 @@
     lax.fori_loop(0, uh_ref.shape[1] // CB, step, 0)
 
 
-def pass2_kernel(n_t, ex1, t2, uh_ref, token, pay, log_a, scr, acc, gain):
+def pass2_kernel(peers, n_t, ex1, t2, uh_ref, pay, log_a, scr, acc, gain):
     la = jnp.log(total_of(ex1, 0, n_t)) * -LOG2E
     log_a[...] = la
     gain[...] = spread(la)
-    pay[n_t : n_t + 16, :] = total_of(ex1, n_t, 16)
+    e1 = total_of(ex1, n_t, 16)
     balance(t2, uh_ref, gain, scr, acc, None, None, 0)
-    pay[0:n_t, :] = lane_sums(acc, n_t)
+    sums = lane_sums(acc, n_t)
+    for p in range(peers):
+        pay[p, 0:n_t, :] = sums
+        pay[p, n_t : n_t + 16, :] = e1
 
 
 def own_rows(nz, th, g):
@@ -249,7 +253,7 @@
     return [pl.multiple_of(((2 * x + c) * nz + z) * th, th) for c in range(g)]
 
 
-def pass3_kernel(nz, th, n_t, ex2, log_a1, t2, uh_ref, pay, log_a2, b_out, scr, acc, gain):
+def pass3_kernel(nz, th, n_t, ex2, log_a1, t2, uh_ref, token, pay, log_a2, b_out, scr, acc, gain):
     la = log_a1[...] - jnp.log(total_of(ex2, 0, n_t)) * LOG2E
     log_a2[...] = la
     gain[...] = spread(la)
@@ -267,8 +271,8 @@
 
 def final_kernel(
     nz, nx, own, th, sh, n_t, n_s,
-    ex3, log_a2, b_ref, t2, uh_ref, late, other, d1, ex1, ex2, student, image, kind, norm, mine,
-    gp, gs, gain, ma, s_scr, d_scr, scr,
+    ex3, log_a2, b_ref, t2, uh_ref, late, other, ex1, ex2, student, image, kind,
+    d2_out, gs, gain, ma, s_scr, scr,
 ):
     x, z = lax.axis_index("x"), lax.axis_index("z")
     peers = ex3.shape[0]
@@ -291,11 +295,6 @@
         g, q = (i * 128) // half_rows, (i * 128) % half_rows
         mixed = jnp.where(core == g % 2, late[g // 2, q : q + 128, :], other[g // 2, q : q + 128, :])
         ma[:, i * 128 : (i + 1) * 128] = (mixed * gain[i * 128 : (i + 1) * 128, :]).T.astype(BF16)
-    total = d1[0]
-    for k in range(1, nz):
-        total = total + d1[k]
-    d_scr[...] = total
-    n_c = uh_ref.shape[1] // 128
     start = (z * nx + x) * own
     n = uh_ref.shape[1] // CB
 
@@ -311,17 +310,8 @@
         dots2 = jnp.sum(uh_ref[:, cols].astype(F32) * d2, axis=0, keepdims=True)
         row = lax.broadcasted_iota(jnp.int32, d2.shape, 0)
 
-        def early(i):
-            return jnp.concatenate(
-                [d_scr[pl.ds(i * n_c + j * (CB // 128) + k, 1), :] for k in range(CB // 128)], axis=1
-            )
-
-        dots = early(own) - dots2
-        outs = []
-        for i in range(own):
-            late = jnp.sum(jnp.where(row == start + i, d2, 0.0), axis=0, keepdims=True)
-            outs.append((early(i) - late - mine[i : i + 1, cols] * dots) / norm[:, cols])
-        gp[:, cols] = jnp.concatenate(outs, axis=0)
+        outs = [jnp.sum(jnp.where(row == start + i, d2, 0.0), axis=0, keepdims=True) for i in range(own)]
+        d2_out[:, cols] = jnp.concatenate(outs + [dots2], axis=0)
 
     fill(0, 0)
 
@@ -336,6 +326,19 @@
     fill(n - 1, 1)
     use(n - 2, 0)
     use(n - 1, 1)
+
+
+def join_kernel(own, d1, d2, norm, mine, gp, d_scr):
+    total = d1[0]
+    for k in range(1, d1.shape[0]):
+        total = total + d1[k]
+    d_scr[...] = total
+    n_c = norm.shape[1] // 128
+    for k in range(n_c):
+        cols = slice(k * 128, (k + 1) * 128)
+        dots = d_scr[own * n_c + k : own * n_c + k + 1, :] - d2[own : own + 1, cols]
+        early = jnp.concatenate([d_scr[i * n_c + k : i * n_c + k + 1, :] for i in range(own)], axis=0)
+        gp[:, cols] = (early - d2[0:own, cols] - mine[:, cols] * dots) / norm[:, cols]
 
 
 def sds(shape, dtype=F32):
@@ -358,9 +361,9 @@
     image, kind = crop_image.reshape(1, crops), crop_kind.reshape(1, crops)
     fl = 2 * teachers * cols * 256
 
-    zp, sp = call(
+    zp = call(
         functools.partial(prep_kernel, nz),
-        (sds((nz, 2 * th, BOT)), sds((sh, BOT))),
+        sds((nz, 2 * th, BOT)),
         student_feat,
         teacher_feat,
         image,
@@ -378,7 +381,7 @@
         functools.partial(pack_kernel, nz, nx),
         (sds((nx, nz * th + sh, BOT)), sds((nx, nz * th, BOT))),
         got,
-        sp,
+        student_feat,
     )
     near = swap(near, "x")
     near_other = lax.ppermute(near, "c", [(0, 1), (1, 0)])
@@ -396,6 +399,16 @@
         flops=fl,
     )
     ex1 = swap(pay1, ("y", "c"))
+    pay2, log_a1 = call(
+        functools.partial(pass2_kernel, peers, n_t),
+        (sds((peers, n_t + 16, 128)), sds((n_t, 128))),
+        ex1,
+        t2,
+        half,
+        scratch=big + [pltpu.VMEM((teachers, 128), F32)],
+        flops=fl // 4,
+    )
+    ex2 = swap(pay2, ("y", "c"))
     d1, token = call(
         functools.partial(student_kernel, nz, nx, own, n_t, n_s),
         (sds((nz * (own + 1) * cols // 128, 128)), sds((8, 128))),
@@ -403,21 +416,11 @@
         s_half,
         half,
         late,
+        log_a1,
         scratch=[pltpu.VMEM((gathered, 128), F32), pltpu.VMEM((gathered, CB), BF16)],
         flops=fl // 2,
     )
     d1 = swap(d1.reshape(nz, (own + 1) * cols // 128, 128), "z")
-    pay2, log_a1 = call(
-        functools.partial(pass2_kernel, n_t),
-        (sds((n_t + 16, 128)), sds((n_t, 128))),
-        ex1,
-        t2,
-        half,
-        token,
-        scratch=big + [pltpu.VMEM((teachers, 128), F32)],
-        flops=fl // 4,
-    )
-    ex2 = lax.all_gather(pay2, ("y", "c"))
     pay3, log_a2, b3 = call(
         functools.partial(pass3_kernel, nz, th, n_t),
         (sds((n_t + teach, 128)), sds((n_t, 128)), sds((1, cols))),
@@ -425,23 +428,33 @@
         log_a1,
         t2,
         half,
+        token,
         scratch=big + [pltpu.VMEM((teachers, 128), F32)],
         flops=fl // 4,
     )
     ex3 = lax.all_gather(pay3, ("y", "c"))
-    return call(
+    d2, grad_student = call(
         functools.partial(final_kernel, nz, nx, own, th, sh, n_t, n_s),
-        (sds((own, cols)), sds((crops, BOT))),
-        ex3, log_a2, b3, t2, half, late, late_other, d1, ex1, ex2, student_feat, image, kind, norm, mine,
+        (sds((own + 1, cols)), sds((crops, BOT))),
+        ex3, log_a2, b3, t2, half, late, late_other, ex1, ex2, student_feat, image, kind,
         scratch=[
             pltpu.VMEM((teachers, 128), F32),
             pltpu.VMEM((BOT, teachers), BF16),
             pltpu.VMEM((gathered, 128), F32),
-            pltpu.VMEM(((own + 1) * cols // 128, 128), F32),
             pltpu.VMEM((2, teachers, CB), BF16),
         ],
         flops=fl * 2,
     )
+    grad_proto = call(
+        functools.partial(join_kernel, own),
+        sds((own, cols)),
+        d1,
+        d2,
+        norm,
+        mine,
+        scratch=[pltpu.VMEM(((own + 1) * cols // 128, 128), F32)],
+    )
+    return grad_proto, grad_student
 
 
 def build(devices):

time: 172 us -> 167 us (0.971)
  blocking collectives: 95.5 us -> 78.5 us
  waiting for transfers between devices: 0.01 us -> 8.94 us
  starting transfers between devices: 22.6 us -> 26.5 us
  local copies, waits for them, and re-layouts: 8.25 us -> 5.81 us
    all_gather x1 -> x0, blocking collectives: 15.4 us -> none  [per_device(): ex2 = lax.all_gather(pay2, ('y', 'c'))]
    all_to_all x2 -> x3, waiting for transfers between devices: 0.01 us -> 8.93 us  [swap(): return lax.all_to_all(x, axes, 0, 0, tiled=True)]
    all_to_all x2 -> x3, starting transfers between devices: 11.2 us -> 14.9 us  [swap(): return lax.all_to_all(x, axes, 0, 0, tiled=True)]
    unnamed x22 -> x16, local copies, waits for them, and re-layouts: 8.25 us -> 5.81 us
    pallas_call x8 -> x9, Pallas kernels: 44.4 us -> 45.3 us  [call(): pl.pallas_call(kernel, out_shape=out_shape, in_specs=[specs] * len(args),...]
  transfers between devices with their start and end apart: 4 -> 5, of which waited for: 0 -> 3; matrix products, arithmetic and copies ran while one was open for 0% -> 0% of each run, Pallas kernels for 16% -> 20%
where the time goes in v3:
time: 167 us; the launch traced here: 166 us
  blocking collectives  78.5 us (47%)
  Pallas kernels  45.3 us (27%)
  starting transfers between devices  26.5 us (16%)
  waiting for transfers between devices  8.94 us (5%)
  local copies, waits for them, and re-layouts  5.81 us (3%)
    all_to_all x3, blocking collectives, swap(): return lax.all_to_all(x, axes, 0, 0, tiled=True)  62.9 us
    pallas_call x9, Pallas kernels, call(): pl.pallas_call(kernel, out_shape=out_shape, in_specs=[specs] * len(args),...  45.3 us
    all_gather x1, blocking collectives, per_device(): ex3 = lax.all_gather(pay3, ('y', 'c'))  15.6 us
    all_to_all x3, starting transfers between devices, swap(): return lax.all_to_all(x, axes, 0, 0, tiled=True)  14.9 us
    ppermute x1, starting transfers between devices, per_device(): near_other = lax.ppermute(near, 'c', [(0, 1), (1, 0)])  9.51 us
    all_to_all x3, waiting for transfers between devices, swap(): return lax.all_to_all(x, axes, 0, 0, tiled=True)  8.93 us
    unnamed x16, local copies, waits for them, and re-layouts  5.81 us
  transfers between devices with their start and end apart: 5, of which 3 were waited for; matrix products, arithmetic and copies ran while one was open for 0% of the time, Pallas kernels for 20%

profile of v3, /device:TPU:1, one launch (start us, length us, event | category | flops | bytes accessed | tf_op | source)
XLA Modules:
  0.0 165.8 jit_solution(17672777838947016902)
XLA Ops:
  0.6 1.8 %shard_map.68 = f32[16,32,128]{2,1,0:T(8,128)} custom-call(bf16[160,128]{1,0:T(8,128)(2,1)} %student.5, bf16[32,128]{1,0:T(8,128)(2,1)} %teacher.1, s32[1,160]{1,0:T(1,128)} %bitcast.5, s32[1,160]{1,0:T(1,128)} %bitcast.7), custom_call_target="tpu_custom_call" | custom-call | tf_op jit(solution)/shard_map/pallas_call | solution.py:34
  2.4 32.5 %all_to_all.30.got = f32[16,32,128]{2,1,0:T(8,128)S(1)} all-to-all(f32[16,32,128]{2,1,0:T(8,128)} %shard_map.68), channel_id=1, replica_groups=mesh['z'=16,'x'=4,'y'=8,'c'=2] {'z'}, dimensions={0} | all-to-all | bytes 524288 | tf_op jit(solution)/shard_map/all_to_all | solution.py:349
  34.9 0.0 copy-start
  34.9 0.8 copy-done
  35.7 0.9 shard_map.69
  36.6 11.6 %all_to_all.31.near = f32[4,336,128]{2,1,0:T(8,128)S(1)} all-to-all(f32[4,336,128]{2,1,0:T(8,128)S(1)} %get-tuple-element.19), channel_id=1, replica_groups=mesh['z'=16,'x'=4,'y'=8,'c'=2] {'x'}, dimensions={0} | all-to-all | bytes 1376256 | tf_op jit(solution)/shard_map/all_to_all | solution.py:349
  48.2 9.5 %collective-permute-start = (f32[4,336,128]{2,1,0:T(8,128)S(1)}, f32[4,336,128]{2,1,0:T(8,128)S(1)}, u32[]{:S(2)}, u32[]{:S(2)}) collective-permute-start(f32[4,336,128]{2,1,0:T(8,128)S(1)} %all_to_all.31.near), channel_id=1, source_target_pairs={{0,1},{1,0},{2,3},{3,2},{4,5},{5,4},{6,7},{7,6},{8,9},{9,8},{10,11... | collective-permute-start | bytes 2064392 | tf_op jit(solution)/shard_map/ppermute | solution.py:387
  57.7 0.0 copy-start.4
  57.7 1.6 copy-done.4
  59.3 0.9 shard_map.70
  60.2 0.0 collective-permute-done.other
  60.3 9.6 %shard_map.71 = (bf16[2048,256]{1,0:T(8,128)(2,1)S(1)}, bf16[640,128]{1,0:T(8,128)(2,1)S(1)}, f32[16,32,128]{2,1,0:T(8,128)S(1)}) custom-call(f32[4,336,128]{2,1,0:T(8,128)S(1)} %all_to_all.31.near, f32[4,336,128]{2,1,0:T(8,128)S(1)} %collective-permute-done.other, bf16[128,4096]{1,0:T(8,128)(2,1)S(1)} %get-tuple-element.20.uh_ref), custom_call_target="tpu_custom_call" | custom-call | flops 4294967296 | tf_op jit(solution)/shard_map/pallas_call | solution.py:34
  69.9 0.0 copy-start.5
  69.9 1.0 copy-done.5
  70.9 18.7 %all_to_all.32.ex1 = f32[16,32,128]{2,1,0:T(8,128)S(1)} all-to-all(f32[16,32,128]{2,1,0:T(8,128)S(1)} %get-tuple-element.21), channel_id=1, replica_groups=mesh['z'=16,'x'=4,'y'=8,'c'=2] {'y','c'}, dimensions={0} | all-to-all | bytes 524288 | tf_op jit(solution)/shard_map/all_to_all | solution.py:349
  89.6 3.5 %all-to-all-start.3 = ((f32[4,256,128]{2,1,0:T(8,128)}), f32[4,256,128]{2,1,0:T(8,128)S(1)}, u32[]{:S(2)}, u32[]{:S(2)}) async-start(f32[4,256,128]{2,1,0:T(8,128)} %get-tuple-element.23), calls=%async_computation.3 | async-start | bytes 1048576 | tf_op jit(solution)/shard_map/all_to_all | solution.py:349
  93.1 0.0 copy-start.6
  93.1 1.2 copy-done.6
  94.3 8.1 %shard_map.72 = (f32[16,32,128]{2,1,0:T(8,128)}, f32[16,128]{1,0:T(8,128)S(1)}) custom-call(f32[16,32,128]{2,1,0:T(8,128)S(1)} %all_to_all.32.ex1, bf16[2048,256]{1,0:T(8,128)(2,1)S(1)} %copy-done.6, bf16[128,4096]{1,0:T(8,128)(2,1)S(1)} %get-tuple-element.20.uh_ref), custom_call_target="tpu_custom_call" | custom-call | flops 1073741824 | tf_op jit(solution)/shard_map/pallas_call | solution.py:34
  102.4 0.7 all-to-all-done.3.late
  103.1 3.7 %all-to-all-start.5 = ((f32[16,32,128]{2,1,0:T(8,128)}), f32[16,32,128]{2,1,0:T(8,128)S(1)}, u32[]{:S(2)}, u32[]{:S(2)}) async-start(f32[16,32,128]{2,1,0:T(8,128)} %get-tuple-element.27), calls=%async_computation.5 | async-start | bytes 524288 | tf_op jit(solution)/shard_map/all_to_all | solution.py:349
  106.8 5.7 %shard_map.73 = (f32[1536,128]{1,0:T(8,128)}, f32[8,128]{1,0:T(8,128)S(1)}) custom-call(f32[16,32,128]{2,1,0:T(8,128)S(1)} %all_to_all.32.ex1, bf16[640,128]{1,0:T(8,128)(2,1)S(1)} %get-tuple-element.22.s_half, bf16[128,4096]{1,0:T(8,128)(2,1)S(1)} %get-tuple-element.20.uh_ref, f32[4,256,128]{2,1,0:T(8,128)S(1)} %all-to-all-done.3.late, ...), custom_call_target="tpu_custom_call" | custom-call | flops 2147483648 | tf_op jit(solution)/shard_map/pallas_call | solution.py:34
  112.5 6.1 %all-to-all-done.5.ex2 = f32[16,32,128]{2,1,0:T(8,128)S(1)} async-done(((f32[16,32,128]{2,1,0:T(8,128)}), f32[16,32,128]{2,1,0:T(8,128)S(1)}, u32[]{:S(2)}, u32[]{:S(2)}) %all-to-all-start.5) | async-done | bytes 262176 | tf_op jit(solution)/shard_map/all_to_all | solution.py:349
  118.7 7.7 %all-to-all-start.4 = ((f32[16,96,128]{2,1,0:T(8,128)}), f32[16,96,128]{2,1,0:T(8,128)S(1)}, u32[]{:S(2)}, u32[]{:S(2)}) async-start(f32[16,96,128]{2,1,0:T(8,128)} %bitcast.2), calls=%async_computation.4 | async-start | bytes 1572864 | tf_op jit(solution)/shard_map/all_to_all | solution.py:349
  126.4 2.1 %collective-permute-start.1 = (f32[4,256,128]{2,1,0:T(8,128)S(1)}, f32[4,256,128]{2,1,0:T(8,128)S(1)}, u32[]{:S(2)}, u32[]{:S(2)}) collective-permute-start(f32[4,256,128]{2,1,0:T(8,128)S(1)} %all-to-all-done.3.late), channel_id=1, source_target_pairs={{0,1},{1,0},{2,3},{3,2},{4,5},{5,4},{6,7},{7,6},{8,9},{9,8},{10,11... | collective-permute-start | bytes 1572872 | tf_op jit(solution)/shard_map/ppermute | solution.py:389
  128.5 0.0 copy-start.7
  128.5 1.2 copy-done.7
  129.7 0.0 copy-start.1
  129.7 0.0 copy-start.2
  129.7 0.0 copy-start.3
  129.7 9.3 %shard_map.74 = (f32[48,128]{1,0:T(8,128)S(1)}, f32[16,128]{1,0:T(8,128)S(1)}, f32[1,4096]{1,0:T(1,128)S(1)}) custom-call(f32[16,32,128]{2,1,0:T(8,128)S(1)} %all-to-all-done.5.ex2, f32[16,128]{1,0:T(8,128)S(1)} %get-tuple-element.25.log_a1, bf16[2048,256]{1,0:T(8,128)(2,1)S(1)} %copy-done.7, bf16[128,4096]{1,0:T(8,128)(2,1)S(1)} %get-tuple-element.20.uh_ref, ...), custom_call_target="tpu_custom_call" | custom-call | flops 1073741824 | tf_op jit(solution)/shard_map/pallas_call | solution.py:34
  139.0 15.6 %all-gather = f32[768,128]{1,0:T(8,128)S(1)} all-gather(f32[48,128]{1,0:T(8,128)S(1)} %get-tuple-element.29), channel_id=2, replica_groups=mesh['z'=16,'x'=4,'y'=8,'c'=2] {'y','c'}, dimensions={0}, use_global_device_ids=true | all-gather | bytes 417792 | tf_op jit(solution)/shard_map/all_gather | solution.py:435
  154.6 0.0 collective-permute-done.1.other
  154.6 0.0 copy-done.1
  154.6 0.0 copy-done.2
  154.6 0.0 copy-done.3
  154.6 8.3 %shard_map.75 = (f32[3,4096]{1,0:T(4,128)S(1)}, f32[160,128]{1,0:T(8,128)}) custom-call(f32[16,48,128]{2,1,0:T(8,128)S(1)} %bitcast.4, f32[16,128]{1,0:T(8,128)S(1)} %get-tuple-element.30.log_a2, f32[1,4096]{1,0:T(1,128)S(1)} %get-tuple-element.31.b_ref, bf16[2048,256]{1,0:T(8,128)(2,1)S(1)} %copy-done.7, bf16[128,4096]{1,0:T(8,128)(2,1)S(1)} %get-tuple-element.20.uh_ref, ...), custom_call_target="tpu_custom_call" | custom-call | flops 8589934592 | tf_op jit(solution)/shard_map/pallas_call | solution.py:34
  163.0 2.2 %all-to-all-done.4.d1 = f32[16,96,128]{2,1,0:T(8,128)S(1)} async-done(((f32[16,96,128]{2,1,0:T(8,128)}), f32[16,96,128]{2,1,0:T(8,128)S(1)}, u32[]{:S(2)}, u32[]{:S(2)}) %all-to-all-start.4) | async-done | bytes 786464 | tf_op jit(solution)/shard_map/all_to_all | solution.py:349
  165.1 0.7 shard_map.76
Async XLA Ops:
  34.9 0.8 copy-start
  48.2 12.1 %collective-permute-start = (f32[4,336,128]{2,1,0:T(8,128)S(1)}, f32[4,336,128]{2,1,0:T(8,128)S(1)}, u32[]{:S(2)}, u32[]{:S(2)}) collective-permute-start(f32[4,336,128]{2,1,0:T(8,128)S(1)} %all_to_all.31.near), channel_id=1, source_target_pairs={{0,1},{1,0},{2,3},{3,2},{4,5},{5,4},{6,7},{7,6},{8,9},{9,8},{10,11... | collective-permute-start | bytes 2064392 | tf_op jit(solution)/shard_map/ppermute | solution.py:387
  57.7 1.6 copy-start.4
  69.9 1.0 copy-start.5
  89.6 13.4 %all-to-all-start.3 = ((f32[4,256,128]{2,1,0:T(8,128)}), f32[4,256,128]{2,1,0:T(8,128)S(1)}, u32[]{:S(2)}, u32[]{:S(2)}) async-start(f32[4,256,128]{2,1,0:T(8,128)} %get-tuple-element.23), calls=%async_computation.3 | async-start | bytes 1048576 | tf_op jit(solution)/shard_map/all_to_all | solution.py:349
  93.1 1.2 copy-start.6
  103.1 15.6 %all-to-all-start.5 = ((f32[16,32,128]{2,1,0:T(8,128)}), f32[16,32,128]{2,1,0:T(8,128)S(1)}, u32[]{:S(2)}, u32[]{:S(2)}) async-start(f32[16,32,128]{2,1,0:T(8,128)} %get-tuple-element.27), calls=%async_computation.5 | async-start | bytes 524288 | tf_op jit(solution)/shard_map/all_to_all | solution.py:349
  118.7 46.4 %all-to-all-start.4 = ((f32[16,96,128]{2,1,0:T(8,128)}), f32[16,96,128]{2,1,0:T(8,128)S(1)}, u32[]{:S(2)}, u32[]{:S(2)}) async-start(f32[16,96,128]{2,1,0:T(8,128)} %bitcast.2), calls=%async_computation.4 | async-start | bytes 1572864 | tf_op jit(solution)/shard_map/all_to_all | solution.py:349
  126.4 28.2 %collective-permute-start.1 = (f32[4,256,128]{2,1,0:T(8,128)S(1)}, f32[4,256,128]{2,1,0:T(8,128)S(1)}, u32[]{:S(2)}, u32[]{:S(2)}) collective-permute-start(f32[4,256,128]{2,1,0:T(8,128)S(1)} %all-to-all-done.3.late), channel_id=1, source_target_pairs={{0,1},{1,0},{2,3},{3,2},{4,5},{5,4},{6,7},{7,6},{8,9},{9,8},{10,11... | collective-permute-start | bytes 1572872 | tf_op jit(solution)/shard_map/ppermute | solution.py:389
  128.5 1.2 copy-start.7
  129.7 24.9 %copy-start.1 = (bf16[160,128]{1,0:T(8,128)(2,1)S(1)}, bf16[160,128]{1,0:T(8,128)(2,1)}, u32[]{:S(2)}) copy-start(bf16[160,128]{1,0:T(8,128)(2,1)} %student.5) | copy-start | bytes 122884
  129.7 24.9 %copy-start.2 = (s32[160]{0:T(256)S(1)}, s32[160]{0:T(256)}, u32[]{:S(2)}) copy-start(s32[160]{0:T(256)} %param.8) | copy-start | bytes 1924
  129.7 24.9 %copy-start.3 = (s32[160]{0:T(256)S(1)}, s32[160]{0:T(256)}, u32[]{:S(2)}) copy-start(s32[160]{0:T(256)} %param.9) | copy-start | bytes 1924

commit v4 on v3

--- a/solution.py
+++ b/solution.py
@@ -100,15 +100,15 @@
     lax.fori_loop(0, proto.shape[1] // CB, step, 0)
 
 
-def pack_kernel(nz, nx, got, student, near, late):
+def pack_kernel(nz, nx, got, student, near):
     th, sh = got.shape[1] // 2, student.shape[0] // 2
     s_unit = row_unit(student[...].astype(F32))[0]
     sp = jnp.where(lax.axis_index("c") == 0, s_unit[:sh], s_unit[sh:])
     for p in range(nx):
         for z in range(nz):
             near[p, z * th : (z + 1) * th, :] = got[z, 0:th, :]
-            late[p, z * th : (z + 1) * th, :] = got[z, th : 2 * th, :]
-        near[p, nz * th :, :] = sp
+            near[p, (nz + z) * th : (nz + z + 1) * th, :] = got[z, th : 2 * th, :]
+        near[p, 2 * nz * th :, :] = sp
 
 
 def powers(t2, u2, gain, r):
@@ -160,7 +160,7 @@
     return half(n, 1, None, b, carry)[1]
 
 
-def pass1_kernel(nz, nx, peers, th, sh, near, other, uh_ref, t2, s_half, pay, scr, acc, es_scr, s_acc):
+def pass1_kernel(nz, nx, peers, th, sh, near, other, uh_ref, t2, s_half, mixed, pay, scr, acc, es_scr, s_acc):
     rows_t = nz * th
     core = lax.axis_index("c")
     for g in range(2 * nx):
@@ -169,7 +169,8 @@
         hi = t.astype(BF16)
         t2[g * rows_t : (g + 1) * rows_t, 0:BOT] = hi
         t2[g * rows_t : (g + 1) * rows_t, BOT : 2 * BOT] = (t - hi.astype(F32)).astype(BF16)
-        s_half[g * sh : (g + 1) * sh, :] = both[rows_t:].astype(BF16)
+        mixed[g * rows_t : (g + 1) * rows_t, :] = both[rows_t : 2 * rows_t]
+        s_half[g * sh : (g + 1) * sh, :] = both[2 * rows_t :].astype(BF16)
     s_acc[...] = jnp.zeros_like(s_acc)
     n_t, n_s = t2.shape[0] // 128, s_half.shape[0] // 128
     own = pl.multiple_of(lax.axis_index("x") * 2 * sh, 2 * sh)
@@ -199,7 +200,7 @@
     return total
 
 
-def student_kernel(nz, nx, own, n_t, n_s, ex1, s_half, uh_ref, late, log_a1, out, token, scale, prob_scr):
+def student_kernel(nz, nx, own, n_t, n_s, ex1, s_half, uh_ref, log_a1, out, token, scale, prob_scr):
     token[...] = jnp.zeros_like(token)
     scale[...] = spread(GRAD_GAIN / total_of(ex1, n_t, 16)[10 : 10 + n_s])
     shape = (nz * own, BOT)
@@ -271,7 +272,7 @@
 
 def final_kernel(
     nz, nx, own, th, sh, n_t, n_s,
-    ex3, log_a2, b_ref, t2, uh_ref, late, other, ex1, ex2, student, image, kind,
+    ex3, log_a2, b_ref, t2, uh_ref, mixed, ex1, ex2, student, image, kind,
     d2_out, gs, gain, ma, s_scr, scr,
 ):
     x, z = lax.axis_index("x"), lax.axis_index("z")
@@ -289,12 +290,9 @@
     s_unit, s_norm = row_unit(student[...].astype(F32))
     gs[...] = (dz - s_unit * jnp.sum(s_unit * dz, axis=1, keepdims=True)) / s_norm
     gain[...] = spread(jnp.exp2(log_a2[...]) * ratio)
-    half_rows = late.shape[1]
-    core = lax.axis_index("c")
     for i in range(n_t):
-        g, q = (i * 128) // half_rows, (i * 128) % half_rows
-        mixed = jnp.where(core == g % 2, late[g // 2, q : q + 128, :], other[g // 2, q : q + 128, :])
-        ma[:, i * 128 : (i + 1) * 128] = (mixed * gain[i * 128 : (i + 1) * 128, :]).T.astype(BF16)
+        rows = slice(i * 128, (i + 1) * 128)
+        ma[:, rows] = (mixed[rows, :] * gain[rows, :]).T.astype(BF16)
     start = (z * nx + x) * own
     n = uh_ref.shape[1] // CB
 
@@ -377,23 +375,21 @@
         flops=fl // 2,
     )
     got = swap(zp, "z")
-    near, late = call(
+    near = call(
         functools.partial(pack_kernel, nz, nx),
-        (sds((nx, nz * th + sh, BOT)), sds((nx, nz * th, BOT))),
+        sds((nx, 2 * nz * th + sh, BOT)),
         got,
         student_feat,
     )
     near = swap(near, "x")
-    near_other = lax.ppermute(near, "c", [(0, 1), (1, 0)])
-    late = swap(late, "x")
-    late_other = lax.ppermute(late, "c", [(0, 1), (1, 0)])
+    other = lax.ppermute(near, "c", [(0, 1), (1, 0)])
 
     big = [pltpu.VMEM((2, teachers, CB), F32), pltpu.VMEM((teachers, 128), F32)]
-    t2, s_half, pay1 = call(
+    t2, s_half, mixed, pay1 = call(
         functools.partial(pass1_kernel, nz, nx, peers, th, sh),
-        (sds((teachers, 256), BF16), sds((gathered, BOT), BF16), sds((peers, n_t + 16, 128))),
+        (sds((teachers, 256), BF16), sds((gathered, BOT), BF16), sds((teachers, BOT)), sds((peers, n_t + 16, 128))),
         near,
-        near_other,
+        other,
         half,
         scratch=big + [pltpu.VMEM((gathered, CB), F32), pltpu.VMEM((gathered, 128), F32)],
         flops=fl,
@@ -415,7 +411,6 @@
         ex1,
         s_half,
         half,
-        late,
         log_a1,
         scratch=[pltpu.VMEM((gathered, 128), F32), pltpu.VMEM((gathered, CB), BF16)],
         flops=fl // 2,
@@ -436,7 +431,7 @@
     d2, grad_student = call(
         functools.partial(final_kernel, nz, nx, own, th, sh, n_t, n_s),
         (sds((own + 1, cols)), sds((crops, BOT))),
-        ex3, log_a2, b3, t2, half, late, late_other, ex1, ex2, student_feat, image, kind,
+        ex3, log_a2, b3, t2, half, mixed, ex1, ex2, student_feat, image, kind,
         scratch=[
             pltpu.VMEM((teachers, 128), F32),
             pltpu.VMEM((BOT, teachers), BF16),

time: 167 us -> 163 us (0.976)
  local copies, waits for them, and re-layouts: 5.81 us -> 0.81 us
  blocking collectives: 78.5 us -> 81.8 us
  starting transfers between devices: 26.5 us -> 23.4 us
    unnamed x16 -> x14, local copies, waits for them, and re-layouts: 5.81 us -> 0.81 us
    all_to_all x3, blocking collectives: 62.9 us -> 66.1 us  [swap(): return lax.all_to_all(x, axes, 0, 0, tiled=True)]
    ppermute x2 -> x1, starting transfers between devices: 11.6 us -> 9.51 us  [per_device(): other = lax.ppermute(near, 'c', [(0, 1), (1, 0)])]
    all_to_all x3 -> x2, starting transfers between devices: 14.9 us -> 13.9 us  [swap(): return lax.all_to_all(x, axes, 0, 0, tiled=True)]
    all_to_all x3 -> x2, waiting for transfers between devices: 8.93 us -> 8.94 us  [swap(): return lax.all_to_all(x, axes, 0, 0, tiled=True)]
  transfers between devices with their start and end apart: 5 -> 3, of which waited for: 3 -> 3; matrix products, arithmetic and copies ran while one was open for 0% -> 0% of each run, Pallas kernels for 20% -> 15%
where the time goes in v4:
time: 163 us; the launch traced here: 162 us
  blocking collectives  81.8 us (50%)
  Pallas kernels  44.6 us (27%)
  starting transfers between devices  23.4 us (14%)
  waiting for transfers between devices  10.5 us (6%)
    all_to_all x3, blocking collectives, swap(): return lax.all_to_all(x, axes, 0, 0, tiled=True)  66.1 us
    pallas_call x9, Pallas kernels, call(): pl.pallas_call(kernel, out_shape=out_shape, in_specs=[specs] * len(args),...  44.6 us
    all_gather x1, blocking collectives, per_device(): ex3 = lax.all_gather(pay3, ('y', 'c'))  15.7 us
    all_to_all x2, starting transfers between devices, swap(): return lax.all_to_all(x, axes, 0, 0, tiled=True)  13.9 us
    ppermute x1, starting transfers between devices, per_device(): other = lax.ppermute(near, 'c', [(0, 1), (1, 0)])  9.51 us
    all_to_all x2, waiting for transfers between devices, swap(): return lax.all_to_all(x, axes, 0, 0, tiled=True)  8.94 us
  transfers between devices with their start and end apart: 3, of which 3 were waited for; matrix products, arithmetic and copies ran while one was open for 0% of the time, Pallas kernels for 15%

profile of v4, /device:TPU:1, one launch (start us, length us, event | category | flops | bytes accessed | tf_op | source)
XLA Modules:
  0.0 161.9 jit_solution(5750985616642219178)
XLA Ops:
  0.6 1.7 %shard_map.68 = f32[16,32,128]{2,1,0:T(8,128)} custom-call(bf16[160,128]{1,0:T(8,128)(2,1)} %student.5, bf16[32,128]{1,0:T(8,128)(2,1)} %teacher.1, s32[1,160]{1,0:T(1,128)} %bitcast.5, s32[1,160]{1,0:T(1,128)} %bitcast.7), custom_call_target="tpu_custom_call" | custom-call | tf_op jit(solution)/shard_map/pallas_call | solution.py:34
  2.4 32.5 %all_to_all.25.got = f32[16,32,128]{2,1,0:T(8,128)S(1)} all-to-all(f32[16,32,128]{2,1,0:T(8,128)} %shard_map.68), channel_id=1, replica_groups=mesh['z'=16,'x'=4,'y'=8,'c'=2] {'z'}, dimensions={0} | all-to-all | bytes 524288 | tf_op jit(solution)/shard_map/all_to_all | solution.py:347
  34.9 0.0 copy-start
  34.9 0.8 copy-done
  35.7 0.1 shard_map.69
  35.8 0.0 copy-start.4
  35.8 14.6 %all_to_all.26.near = f32[4,592,128]{2,1,0:T(8,128)S(1)} all-to-all(f32[4,592,128]{2,1,0:T(8,128)S(1)} %shard_map.69), channel_id=1, replica_groups=mesh['z'=16,'x'=4,'y'=8,'c'=2] {'x'}, dimensions={0} | all-to-all | bytes 2424832 | tf_op jit(solution)/shard_map/all_to_all | solution.py:347
  50.4 9.5 %collective-permute-start = (f32[4,592,128]{2,1,0:T(8,128)S(1)}, f32[4,592,128]{2,1,0:T(8,128)S(1)}, u32[]{:S(2)}, u32[]{:S(2)}) collective-permute-start(f32[4,592,128]{2,1,0:T(8,128)S(1)} %all_to_all.26.near), channel_id=1, source_target_pairs={{0,1},{1,0},{2,3},{3,2},{4,5},{5,4},{6,7},{7,6},{8,9},{9,8},{10,11... | collective-permute-start | bytes 3637256 | tf_op jit(solution)/shard_map/ppermute | solution.py:385
  59.9 0.0 copy-done.4
  59.9 0.9 shard_map.70
  60.9 1.5 collective-permute-done.other
  62.4 9.7 %shard_map.71 = (bf16[2048,256]{1,0:T(8,128)(2,1)S(1)}, bf16[640,128]{1,0:T(8,128)(2,1)S(1)}, f32[2048,128]{1,0:T(8,128)S(1)}, f32[16,32,128]{2,1,0:T(8,128)S(1)}) custom-call(f32[4,592,128]{2,1,0:T(8,128)S(1)} %all_to_all.26.near, f32[4,592,128]{2,1,0:T(8,128)S(1)} %collective-permute-done.other, bf16[128,4096]{1,0:T(8,128)(2,1)S(1)} %get-tuple-element.18.uh_ref), custom_call_target="tpu_custom_call" | custom-call | flops 4294967296 | tf_op jit(solution)/shard_map/pallas_call | solution.py:34
  72.1 0.0 copy-start.5
  72.1 19.0 %all_to_all.27.ex1 = f32[16,32,128]{2,1,0:T(8,128)S(1)} all-to-all(f32[16,32,128]{2,1,0:T(8,128)S(1)} %get-tuple-element.19), channel_id=1, replica_groups=mesh['z'=16,'x'=4,'y'=8,'c'=2] {'y','c'}, dimensions={0} | all-to-all | bytes 524288 | tf_op jit(solution)/shard_map/all_to_all | solution.py:347
  91.1 8.1 %shard_map.72 = (f32[16,32,128]{2,1,0:T(8,128)}, f32[16,128]{1,0:T(8,128)S(1)}) custom-call(f32[16,32,128]{2,1,0:T(8,128)S(1)} %all_to_all.27.ex1, bf16[2048,256]{1,0:T(8,128)(2,1)S(1)} %get-tuple-element.21.t2, bf16[128,4096]{1,0:T(8,128)(2,1)S(1)} %get-tuple-element.18.uh_ref), custom_call_target="tpu_custom_call" | custom-call | flops 1073741824 | tf_op jit(solution)/shard_map/pallas_call | solution.py:34
  99.3 0.0 copy-done.5
  99.3 3.4 %all-to-all-start.4 = ((f32[16,32,128]{2,1,0:T(8,128)}), f32[16,32,128]{2,1,0:T(8,128)S(1)}, u32[]{:S(2)}, u32[]{:S(2)}) async-start(f32[16,32,128]{2,1,0:T(8,128)} %get-tuple-element.24), calls=%async_computation.4 | async-start | bytes 524288 | tf_op jit(solution)/shard_map/all_to_all | solution.py:347
  102.7 5.7 %shard_map.73 = (f32[1536,128]{1,0:T(8,128)}, f32[8,128]{1,0:T(8,128)S(1)}) custom-call(f32[16,32,128]{2,1,0:T(8,128)S(1)} %all_to_all.27.ex1, bf16[640,128]{1,0:T(8,128)(2,1)S(1)} %get-tuple-element.20.s_half, bf16[128,4096]{1,0:T(8,128)(2,1)S(1)} %get-tuple-element.18.uh_ref, f32[16,128]{1,0:T(8,128)S(1)} %get-tuple-element.22.log_a1), custom_call_target="tpu_custom_call" | custom-call | flops 2147483648 | tf_op jit(solution)/shard_map/pallas_call | solution.py:34
  108.4 5.4 %all-to-all-done.4.ex2 = f32[16,32,128]{2,1,0:T(8,128)S(1)} async-done(((f32[16,32,128]{2,1,0:T(8,128)}), f32[16,32,128]{2,1,0:T(8,128)S(1)}, u32[]{:S(2)}, u32[]{:S(2)}) %all-to-all-start.4) | async-done | bytes 262176 | tf_op jit(solution)/shard_map/all_to_all | solution.py:347
  113.8 10.5 %all-to-all-start.3 = ((f32[16,96,128]{2,1,0:T(8,128)}), f32[16,96,128]{2,1,0:T(8,128)S(1)}, u32[]{:S(2)}, u32[]{:S(2)}) async-start(f32[16,96,128]{2,1,0:T(8,128)} %bitcast.2), calls=%async_computation.3 | async-start | bytes 1572864 | tf_op jit(solution)/shard_map/all_to_all | solution.py:347
  124.3 0.0 copy-start.1
  124.4 0.0 copy-start.2
  124.4 0.0 copy-start.3
  124.4 0.0 copy-start.6
  124.4 9.3 %shard_map.74 = (f32[48,128]{1,0:T(8,128)S(1)}, f32[16,128]{1,0:T(8,128)S(1)}, f32[1,4096]{1,0:T(1,128)S(1)}) custom-call(f32[16,32,128]{2,1,0:T(8,128)S(1)} %all-to-all-done.4.ex2, f32[16,128]{1,0:T(8,128)S(1)} %get-tuple-element.22.log_a1, bf16[2048,256]{1,0:T(8,128)(2,1)S(1)} %get-tuple-element.21.t2, bf16[128,4096]{1,0:T(8,128)(2,1)S(1)} %get-tuple-element.18.uh_ref, ...), custom_call_target="tpu_custom_call" | custom-call | flops 1073741824 | tf_op jit(solution)/shard_map/pallas_call | solution.py:34
  133.7 15.7 %all-gather = f32[768,128]{1,0:T(8,128)S(1)} all-gather(f32[48,128]{1,0:T(8,128)S(1)} %get-tuple-element.26), channel_id=2, replica_groups=mesh['z'=16,'x'=4,'y'=8,'c'=2] {'y','c'}, dimensions={0}, use_global_device_ids=true | all-gather | bytes 417792 | tf_op jit(solution)/shard_map/all_gather | solution.py:430
  149.3 0.0 copy-done.1
  149.3 0.0 copy-done.2
  149.3 0.0 copy-done.3
  149.3 0.0 copy-done.6
  149.3 8.3 %shard_map.75 = (f32[3,4096]{1,0:T(4,128)S(1)}, f32[160,128]{1,0:T(8,128)}) custom-call(f32[16,48,128]{2,1,0:T(8,128)S(1)} %bitcast.4, f32[16,128]{1,0:T(8,128)S(1)} %get-tuple-element.27.log_a2, f32[1,4096]{1,0:T(1,128)S(1)} %get-tuple-element.28.b_ref, bf16[2048,256]{1,0:T(8,128)(2,1)S(1)} %get-tuple-element.21.t2, ...), custom_call_target="tpu_custom_call" | custom-call | flops 8589934592 | tf_op jit(solution)/shard_map/pallas_call | solution.py:34
  157.6 3.6 %all-to-all-done.3.d1 = f32[16,96,128]{2,1,0:T(8,128)S(1)} async-done(((f32[16,96,128]{2,1,0:T(8,128)}), f32[16,96,128]{2,1,0:T(8,128)S(1)}, u32[]{:S(2)}, u32[]{:S(2)}) %all-to-all-start.3) | async-done | bytes 786464 | tf_op jit(solution)/shard_map/all_to_all | solution.py:347
  161.2 0.7 shard_map.76
Async XLA Ops:
  34.9 0.8 copy-start
  35.8 24.1 %copy-start.4 = (f32[128,4096]{1,0:T(8,128)S(1)}, f32[128,4096]{1,0:T(8,128)}, u32[]{:S(2)}) copy-start(f32[128,4096]{1,0:T(8,128)} %proto.1) | copy-start | bytes 6291460
  50.4 12.0 %collective-permute-start = (f32[4,592,128]{2,1,0:T(8,128)S(1)}, f32[4,592,128]{2,1,0:T(8,128)S(1)}, u32[]{:S(2)}, u32[]{:S(2)}) collective-permute-start(f32[4,592,128]{2,1,0:T(8,128)S(1)} %all_to_all.26.near), channel_id=1, source_target_pairs={{0,1},{1,0},{2,3},{3,2},{4,5},{5,4},{6,7},{7,6},{8,9},{9,8},{10,11... | collective-permute-start | bytes 3637256 | tf_op jit(solution)/shard_map/ppermute | solution.py:385
  72.1 27.1 %copy-start.5 = (f32[2048,128]{1,0:T(8,128)}, f32[2048,128]{1,0:T(8,128)S(1)}, u32[]{:S(2)}) copy-start(f32[2048,128]{1,0:T(8,128)S(1)} %get-tuple-element.29.mixed) | copy-start | bytes 3145732
  99.3 14.6 %all-to-all-start.4 = ((f32[16,32,128]{2,1,0:T(8,128)}), f32[16,32,128]{2,1,0:T(8,128)S(1)}, u32[]{:S(2)}, u32[]{:S(2)}) async-start(f32[16,32,128]{2,1,0:T(8,128)} %get-tuple-element.24), calls=%async_computation.4 | async-start | bytes 524288 | tf_op jit(solution)/shard_map/all_to_all | solution.py:347
  113.8 47.3 %all-to-all-start.3 = ((f32[16,96,128]{2,1,0:T(8,128)}), f32[16,96,128]{2,1,0:T(8,128)S(1)}, u32[]{:S(2)}, u32[]{:S(2)}) async-start(f32[16,96,128]{2,1,0:T(8,128)} %bitcast.2), calls=%async_computation.3 | async-start | bytes 1572864 | tf_op jit(solution)/shard_map/all_to_all | solution.py:347
  124.3 25.0 %copy-start.1 = (bf16[160,128]{1,0:T(8,128)(2,1)S(1)}, bf16[160,128]{1,0:T(8,128)(2,1)}, u32[]{:S(2)}) copy-start(bf16[160,128]{1,0:T(8,128)(2,1)} %student.5) | copy-start | bytes 122884
  124.4 25.0 %copy-start.2 = (s32[160]{0:T(256)S(1)}, s32[160]{0:T(256)}, u32[]{:S(2)}) copy-start(s32[160]{0:T(256)} %param.8) | copy-start | bytes 1924
  124.4 25.0 %copy-start.3 = (s32[160]{0:T(256)S(1)}, s32[160]{0:T(256)}, u32[]{:S(2)}) copy-start(s32[160]{0:T(256)} %param.9) | copy-start | bytes 1924
  124.4 25.0 %copy-start.6 = (f32[2048,128]{1,0:T(8,128)S(1)}, f32[2048,128]{1,0:T(8,128)}, u32[]{:S(2)}) copy-start(f32[2048,128]{1,0:T(8,128)} %copy-done.5) | copy-start | bytes 3145732

commit v5 on v4

--- a/solution.py
+++ b/solution.py
@@ -160,7 +160,7 @@
     return half(n, 1, None, b, carry)[1]
 
 
-def pass1_kernel(nz, nx, peers, th, sh, near, other, uh_ref, t2, s_half, mixed, pay, scr, acc, es_scr, s_acc):
+def pass1_kernel(nz, nx, peers, th, sh, near, other, uh_ref, t2, s_half, mixed, e1_out, pay, scr, acc, es_scr, s_acc):
     rows_t = nz * th
     core = lax.axis_index("c")
     for g in range(2 * nx):
@@ -185,12 +185,11 @@
 
     e1 = balance(t2, uh_ref, None, scr, acc, first, None, jnp.zeros((2 * sh, BOT), F32))
     sums = lane_sums(acc, n_t)
-    totals = lane_sums(s_acc, n_s)
-    part = 2 * sh // peers
-    fill = jnp.zeros((16 - part - n_s, BOT), F32)
+    totals = jnp.concatenate([lane_sums(s_acc, n_s), jnp.zeros((8 - n_s, 128), F32)], axis=0)
+    e1_out[...] = e1
     for p in range(peers):
         pay[p, 0:n_t, :] = sums
-        pay[p, n_t : n_t + 16, :] = jnp.concatenate([e1[p * part : (p + 1) * part, :], totals, fill], axis=0)
+        pay[p, n_t : n_t + 8, :] = totals
 
 
 def total_of(ref, start, rows):
@@ -202,7 +201,7 @@
 
 def student_kernel(nz, nx, own, n_t, n_s, ex1, s_half, uh_ref, log_a1, out, token, scale, prob_scr):
     token[...] = jnp.zeros_like(token)
-    scale[...] = spread(GRAD_GAIN / total_of(ex1, n_t, 16)[10 : 10 + n_s])
+    scale[...] = spread(GRAD_GAIN / total_of(ex1, n_t, 8)[:n_s])
     shape = (nz * own, BOT)
     row = lax.broadcasted_iota(jnp.int32, shape, 0)
     lane = lax.broadcasted_iota(jnp.int32, shape, 1)
@@ -237,16 +236,17 @@
     lax.fori_loop(0, uh_ref.shape[1] // CB, step, 0)
 
 
-def pass2_kernel(peers, n_t, ex1, t2, uh_ref, pay, log_a, scr, acc, gain):
+def pass2_kernel(peers, n_t, ex1, e1, t2, uh_ref, pay, log_a, scr, acc, gain):
     la = jnp.log(total_of(ex1, 0, n_t)) * -LOG2E
     log_a[...] = la
     gain[...] = spread(la)
-    e1 = total_of(ex1, n_t, 16)
+    part = e1.shape[0] // peers
+    fill = jnp.zeros((16 - part, BOT), F32)
     balance(t2, uh_ref, gain, scr, acc, None, None, 0)
     sums = lane_sums(acc, n_t)
     for p in range(peers):
         pay[p, 0:n_t, :] = sums
-        pay[p, n_t : n_t + 16, :] = e1
+        pay[p, n_t : n_t + 16, :] = jnp.concatenate([e1[p * part : (p + 1) * part, :], fill], axis=0)
 
 
 def own_rows(nz, th, g):
@@ -267,23 +267,24 @@
 
     t_sum = balance(t2, uh_ref, gain, scr, acc, None, finish, jnp.zeros((2 * th, BOT), F32))
     pay[0:n_t, :] = lane_sums(acc, n_t)
-    pay[n_t:, :] = t_sum
+    pay[n_t : n_t + 2 * th, :] = t_sum
+    pay[n_t + 2 * th :, :] = total_of(ex2, n_t, 16)
 
 
 def final_kernel(
     nz, nx, own, th, sh, n_t, n_s,
-    ex3, log_a2, b_ref, t2, uh_ref, mixed, ex1, ex2, student, image, kind,
+    ex3, log_a2, b_ref, t2, uh_ref, mixed, ex1, student, image, kind,
     d2_out, gs, gain, ma, s_scr, scr,
 ):
     x, z = lax.axis_index("x"), lax.axis_index("z")
     peers = ex3.shape[0]
     ratio = 1.0 / total_of(ex3, 0, n_t)
     gain[...] = spread(ratio)
-    s_scr[...] = spread(1.0 / total_of(ex1, n_t, 16)[10 : 10 + n_s])
+    s_scr[...] = spread(1.0 / total_of(ex1, n_t, 8)[:n_s])
     own_ratio = jnp.concatenate([gain[pl.ds(s, th), :] for s in own_rows(nz, th, 2)], axis=0)
     t_sum = total_of(ex3, n_t, 2 * th) * own_ratio
     part = 2 * sh // peers
-    e1 = jnp.concatenate([ex2[p, n_t : n_t + part, :] for p in range(peers)], axis=0)
+    e1 = jnp.concatenate([ex3[p, n_t + 2 * th : n_t + 2 * th + part, :] for p in range(peers)], axis=0)
     e1 = e1 * s_scr[pl.ds(pl.multiple_of(x * 2 * sh, 2 * sh), 2 * sh), :]
     weights = selector(image[...], kind[...], 2 * th)
     dz = GRAD_GAIN * (e1 - mm(weights, t_sum, 0, 0, HI))
@@ -385,9 +386,9 @@
     other = lax.ppermute(near, "c", [(0, 1), (1, 0)])
 
     big = [pltpu.VMEM((2, teachers, CB), F32), pltpu.VMEM((teachers, 128), F32)]
-    t2, s_half, mixed, pay1 = call(
+    t2, s_half, mixed, e1, pay1 = call(
         functools.partial(pass1_kernel, nz, nx, peers, th, sh),
-        (sds((teachers, 256), BF16), sds((gathered, BOT), BF16), sds((teachers, BOT)), sds((peers, n_t + 16, 128))),
+        (sds((teachers, 256), BF16), sds((gathered, BOT), BF16), sds((teachers, BOT)), sds((crops, BOT)), sds((peers, n_t + 8, 128))),
         near,
         other,
         half,
@@ -399,6 +400,7 @@
         functools.partial(pass2_kernel, peers, n_t),
         (sds((peers, n_t + 16, 128)), sds((n_t, 128))),
         ex1,
+        e1,
         t2,
         half,
         scratch=big + [pltpu.VMEM((teachers, 128), F32)],
@@ -418,7 +420,7 @@
     d1 = swap(d1.reshape(nz, (own + 1) * cols // 128, 128), "z")
     pay3, log_a2, b3 = call(
         functools.partial(pass3_kernel, nz, th, n_t),
-        (sds((n_t + teach, 128)), sds((n_t, 128)), sds((1, cols))),
+        (sds((n_t + teach + 16, 128)), sds((n_t, 128)), sds((1, cols))),
         ex2,
         log_a1,
         t2,
@@ -431,7 +433,7 @@
     d2, grad_student = call(
         functools.partial(final_kernel, nz, nx, own, th, sh, n_t, n_s),
         (sds((own + 1, cols)), sds((crops, BOT))),
-        ex3, log_a2, b3, t2, half, mixed, ex1, ex2, student_feat, image, kind,
+        ex3, log_a2, b3, t2, half, mixed, ex1, student_feat, image, kind,
         scratch=[
             pltpu.VMEM((teachers, 128), F32),
             pltpu.VMEM((BOT, teachers), BF16),

time: 163 us -> 163 us (level)
  no operation moved by 1% of the time
where the time goes in v5:
time: 163 us; the launch traced here: 162 us
  blocking collectives  80.6 us (49%)
  Pallas kernels  44.6 us (27%)
  starting transfers between devices  23.5 us (14%)
  waiting for transfers between devices  11.9 us (7%)
    all_to_all x3, blocking collectives, swap(): return lax.all_to_all(x, axes, 0, 0, tiled=True)  64.7 us
    pallas_call x9, Pallas kernels, call(): pl.pallas_call(kernel, out_shape=out_shape, in_specs=[specs] * len(args),...  44.6 us
    all_gather x1, blocking collectives, per_device(): ex3 = lax.all_gather(pay3, ('y', 'c'))  15.9 us
    all_to_all x2, starting transfers between devices, swap(): return lax.all_to_all(x, axes, 0, 0, tiled=True)  14 us
    all_to_all x2, waiting for transfers between devices, swap(): return lax.all_to_all(x, axes, 0, 0, tiled=True)  10.3 us
    ppermute x1, starting transfers between devices, per_device(): other = lax.ppermute(near, 'c', [(0, 1), (1, 0)])  9.51 us
  transfers between devices with their start and end apart: 3, of which 3 were waited for; matrix products, arithmetic and copies ran while one was open for 0% of the time, Pallas kernels for 15%

profile of v5, /device:TPU:1, one launch (start us, length us, event | category | flops | bytes accessed | tf_op | source)
XLA Modules:
  0.0 162.2 jit_solution(14073894595693963170)
XLA Ops:
  0.6 1.7 %shard_map.68 = f32[16,32,128]{2,1,0:T(8,128)} custom-call(bf16[160,128]{1,0:T(8,128)(2,1)} %student.5, bf16[32,128]{1,0:T(8,128)(2,1)} %teacher.1, s32[1,160]{1,0:T(1,128)} %bitcast.5, s32[1,160]{1,0:T(1,128)} %bitcast.7), custom_call_target="tpu_custom_call" | custom-call | tf_op jit(solution)/shard_map/pallas_call | solution.py:34
  2.4 32.5 %all_to_all.25.got = f32[16,32,128]{2,1,0:T(8,128)S(1)} all-to-all(f32[16,32,128]{2,1,0:T(8,128)} %shard_map.68), channel_id=1, replica_groups=mesh['z'=16,'x'=4,'y'=8,'c'=2] {'z'}, dimensions={0} | all-to-all | bytes 524288 | tf_op jit(solution)/shard_map/all_to_all | solution.py:348
  34.9 0.0 copy-start
  34.9 0.8 copy-done
  35.7 0.1 shard_map.69
  35.8 0.0 copy-start.4
  35.8 14.6 %all_to_all.26.near = f32[4,592,128]{2,1,0:T(8,128)S(1)} all-to-all(f32[4,592,128]{2,1,0:T(8,128)S(1)} %shard_map.69), channel_id=1, replica_groups=mesh['z'=16,'x'=4,'y'=8,'c'=2] {'x'}, dimensions={0} | all-to-all | bytes 2424832 | tf_op jit(solution)/shard_map/all_to_all | solution.py:348
  50.4 9.5 %collective-permute-start = (f32[4,592,128]{2,1,0:T(8,128)S(1)}, f32[4,592,128]{2,1,0:T(8,128)S(1)}, u32[]{:S(2)}, u32[]{:S(2)}) collective-permute-start(f32[4,592,128]{2,1,0:T(8,128)S(1)} %all_to_all.26.near), channel_id=1, source_target_pairs={{0,1},{1,0},{2,3},{3,2},{4,5},{5,4},{6,7},{7,6},{8,9},{9,8},{10,11... | collective-permute-start | bytes 3637256 | tf_op jit(solution)/shard_map/ppermute | solution.py:386
  59.9 0.0 copy-done.4
  59.9 0.9 shard_map.70
  60.9 1.5 collective-permute-done.other
  62.4 9.7 %shard_map.71 = (bf16[2048,256]{1,0:T(8,128)(2,1)S(1)}, bf16[640,128]{1,0:T(8,128)(2,1)S(1)}, f32[2048,128]{1,0:T(8,128)S(1)}, f32[160,128]{1,0:T(8,128)S(1)}, f32[16,24,128]{2,1,0:T(8,128)S(1)}) custom-call(f32[4,592,128]{2,1,0:T(8,128)S(1)} %all_to_all.26.near, f32[4,592,128]{2,1,0:T(8,128)S(1)} %collective-permute-done.other, ...), custom_call_target="tpu_custom_call" | custom-call | flops 4294967296 | tf_op jit(solution)/shard_map/pallas_call | solution.py:34
  72.1 0.0 copy-start.5
  72.1 17.6 %all_to_all.27.ex1 = f32[16,24,128]{2,1,0:T(8,128)S(1)} all-to-all(f32[16,24,128]{2,1,0:T(8,128)S(1)} %get-tuple-element.20), channel_id=1, replica_groups=mesh['z'=16,'x'=4,'y'=8,'c'=2] {'y','c'}, dimensions={0} | all-to-all | bytes 393216 | tf_op jit(solution)/shard_map/all_to_all | solution.py:348
  89.7 8.1 %shard_map.72 = (f32[16,32,128]{2,1,0:T(8,128)}, f32[16,128]{1,0:T(8,128)S(1)}) custom-call(f32[16,24,128]{2,1,0:T(8,128)S(1)} %all_to_all.27.ex1, f32[160,128]{1,0:T(8,128)S(1)} %get-tuple-element.22.e1, bf16[2048,256]{1,0:T(8,128)(2,1)S(1)} %get-tuple-element.23.t2, bf16[128,4096]{1,0:T(8,128)(2,1)S(1)} %get-tuple-element.19.uh_ref), custom_call_target="tpu_custom_call" | custom-call | flops 1073741824 | tf_op jit(solution)/shard_map/pallas_call | solution.py:34
  97.8 0.0 copy-done.5
  97.8 3.4 %all-to-all-start.4 = ((f32[16,32,128]{2,1,0:T(8,128)}), f32[16,32,128]{2,1,0:T(8,128)S(1)}, u32[]{:S(2)}, u32[]{:S(2)}) async-start(f32[16,32,128]{2,1,0:T(8,128)} %get-tuple-element.26), calls=%async_computation.4 | async-start | bytes 524288 | tf_op jit(solution)/shard_map/all_to_all | solution.py:348
  101.3 5.7 %shard_map.73 = (f32[1536,128]{1,0:T(8,128)}, f32[8,128]{1,0:T(8,128)S(1)}) custom-call(f32[16,24,128]{2,1,0:T(8,128)S(1)} %all_to_all.27.ex1, bf16[640,128]{1,0:T(8,128)(2,1)S(1)} %get-tuple-element.21.s_half, bf16[128,4096]{1,0:T(8,128)(2,1)S(1)} %get-tuple-element.19.uh_ref, f32[16,128]{1,0:T(8,128)S(1)} %get-tuple-element.24.log_a1), custom_call_target="tpu_custom_call" | custom-call | flops 2147483648 | tf_op jit(solution)/shard_map/pallas_call | solution.py:34
  107.0 5.6 %all-to-all-done.4.ex2 = f32[16,32,128]{2,1,0:T(8,128)S(1)} async-done(((f32[16,32,128]{2,1,0:T(8,128)}), f32[16,32,128]{2,1,0:T(8,128)S(1)}, u32[]{:S(2)}, u32[]{:S(2)}) %all-to-all-start.4) | async-done | bytes 262176 | tf_op jit(solution)/shard_map/all_to_all | solution.py:348
  112.7 10.5 %all-to-all-start.3 = ((f32[16,96,128]{2,1,0:T(8,128)}), f32[16,96,128]{2,1,0:T(8,128)S(1)}, u32[]{:S(2)}, u32[]{:S(2)}) async-start(f32[16,96,128]{2,1,0:T(8,128)} %bitcast.2), calls=%async_computation.3 | async-start | bytes 1572864 | tf_op jit(solution)/shard_map/all_to_all | solution.py:348
  123.2 0.0 copy-start.1
  123.2 0.0 copy-start.2
  123.2 0.0 copy-start.3
  123.2 0.0 copy-start.6
  123.2 9.3 %shard_map.74 = (f32[64,128]{1,0:T(8,128)S(1)}, f32[16,128]{1,0:T(8,128)S(1)}, f32[1,4096]{1,0:T(1,128)S(1)}) custom-call(f32[16,32,128]{2,1,0:T(8,128)S(1)} %all-to-all-done.4.ex2, f32[16,128]{1,0:T(8,128)S(1)} %get-tuple-element.24.log_a1, bf16[2048,256]{1,0:T(8,128)(2,1)S(1)} %get-tuple-element.23.t2, bf16[128,4096]{1,0:T(8,128)(2,1)S(1)} %get-tuple-element.19.uh_ref, ...), custom_call_target="tpu_custom_call" | custom-call | flops 1073741824 | tf_op jit(solution)/shard_map/pallas_call | solution.py:34
  132.5 15.9 %all-gather = f32[1024,128]{1,0:T(8,128)S(1)} all-gather(f32[64,128]{1,0:T(8,128)S(1)} %get-tuple-element.28), channel_id=2, replica_groups=mesh['z'=16,'x'=4,'y'=8,'c'=2] {'y','c'}, dimensions={0}, use_global_device_ids=true | all-gather | bytes 557056 | tf_op jit(solution)/shard_map/all_gather | solution.py:432
  148.4 0.0 copy-done.1
  148.4 0.0 copy-done.2
  148.5 0.0 copy-done.3
  148.5 0.0 copy-done.6
  148.5 8.3 %shard_map.75 = (f32[3,4096]{1,0:T(4,128)S(1)}, f32[160,128]{1,0:T(8,128)}) custom-call(f32[16,64,128]{2,1,0:T(8,128)S(1)} %bitcast.4, f32[16,128]{1,0:T(8,128)S(1)} %get-tuple-element.29.log_a2, f32[1,4096]{1,0:T(1,128)S(1)} %get-tuple-element.30.b_ref, bf16[2048,256]{1,0:T(8,128)(2,1)S(1)} %get-tuple-element.23.t2, ...), custom_call_target="tpu_custom_call" | custom-call | flops 8589934592 | tf_op jit(solution)/shard_map/pallas_call | solution.py:34
  156.7 4.7 %all-to-all-done.3.d1 = f32[16,96,128]{2,1,0:T(8,128)S(1)} async-done(((f32[16,96,128]{2,1,0:T(8,128)}), f32[16,96,128]{2,1,0:T(8,128)S(1)}, u32[]{:S(2)}, u32[]{:S(2)}) %all-to-all-start.3) | async-done | bytes 786464 | tf_op jit(solution)/shard_map/all_to_all | solution.py:348
  161.4 0.7 shard_map.76
Async XLA Ops:
  34.9 0.8 copy-start
  35.8 24.1 %copy-start.4 = (f32[128,4096]{1,0:T(8,128)S(1)}, f32[128,4096]{1,0:T(8,128)}, u32[]{:S(2)}) copy-start(f32[128,4096]{1,0:T(8,128)} %proto.1) | copy-start | bytes 6291460
  50.4 12.0 %collective-permute-start = (f32[4,592,128]{2,1,0:T(8,128)S(1)}, f32[4,592,128]{2,1,0:T(8,128)S(1)}, u32[]{:S(2)}, u32[]{:S(2)}) collective-permute-start(f32[4,592,128]{2,1,0:T(8,128)S(1)} %all_to_all.26.near), channel_id=1, source_target_pairs={{0,1},{1,0},{2,3},{3,2},{4,5},{5,4},{6,7},{7,6},{8,9},{9,8},{10,11... | collective-permute-start | bytes 3637256 | tf_op jit(solution)/shard_map/ppermute | solution.py:386
  72.1 25.7 %copy-start.5 = (f32[2048,128]{1,0:T(8,128)}, f32[2048,128]{1,0:T(8,128)S(1)}, u32[]{:S(2)}) copy-start(f32[2048,128]{1,0:T(8,128)S(1)} %get-tuple-element.31.mixed) | copy-start | bytes 3145732
  97.8 14.8 %all-to-all-start.4 = ((f32[16,32,128]{2,1,0:T(8,128)}), f32[16,32,128]{2,1,0:T(8,128)S(1)}, u32[]{:S(2)}, u32[]{:S(2)}) async-start(f32[16,32,128]{2,1,0:T(8,128)} %get-tuple-element.26), calls=%async_computation.4 | async-start | bytes 524288 | tf_op jit(solution)/shard_map/all_to_all | solution.py:348
  112.7 48.8 %all-to-all-start.3 = ((f32[16,96,128]{2,1,0:T(8,128)}), f32[16,96,128]{2,1,0:T(8,128)S(1)}, u32[]{:S(2)}, u32[]{:S(2)}) async-start(f32[16,96,128]{2,1,0:T(8,128)} %bitcast.2), calls=%async_computation.3 | async-start | bytes 1572864 | tf_op jit(solution)/shard_map/all_to_all | solution.py:348
  123.2 25.2 %copy-start.1 = (bf16[160,128]{1,0:T(8,128)(2,1)S(1)}, bf16[160,128]{1,0:T(8,128)(2,1)}, u32[]{:S(2)}) copy-start(bf16[160,128]{1,0:T(8,128)(2,1)} %student.5) | copy-start | bytes 122884
  123.2 25.2 %copy-start.2 = (s32[160]{0:T(256)S(1)}, s32[160]{0:T(256)}, u32[]{:S(2)}) copy-start(s32[160]{0:T(256)} %param.8) | copy-start | bytes 1924
  123.2 25.2 %copy-start.3 = (s32[160]{0:T(256)S(1)}, s32[160]{0:T(256)}, u32[]{:S(2)}) copy-start(s32[160]{0:T(256)} %param.9) | copy-start | bytes 1924
  123.2 25.2 %copy-start.6 = (f32[2048,128]{1,0:T(8,128)S(1)}, f32[2048,128]{1,0:T(8,128)}, u32[]{:S(2)}) copy-start(f32[2048,128]{1,0:T(8,128)} %copy-done.5) | copy-start | bytes 3145732

commit v6 on v5

--- a/solution.py
+++ b/solution.py
@@ -254,7 +254,7 @@
     return [pl.multiple_of(((2 * x + c) * nz + z) * th, th) for c in range(g)]
 
 
-def pass3_kernel(nz, th, n_t, ex2, log_a1, t2, uh_ref, token, pay, log_a2, b_out, scr, acc, gain):
+def pass3_kernel(nz, th, n_t, ex2, log_a1, t2, uh_ref, token, pay, log_a2, b_out, scr, acc, gain, own_scr):
     la = log_a1[...] - jnp.log(total_of(ex2, 0, n_t)) * LOG2E
     log_a2[...] = la
     gain[...] = spread(la)
@@ -263,9 +263,11 @@
     def finish(j, b, block, uh, t_sum):
         b_out[:, pl.ds(pl.multiple_of(j * CB, CB), CB)] = b
         mine = jnp.concatenate([block[pl.ds(s, th), :] for s in starts], axis=0) * b
-        return t_sum + mm(mine.astype(BF16), uh, 1, 1)
-
-    t_sum = balance(t2, uh_ref, gain, scr, acc, None, finish, jnp.zeros((2 * th, BOT), F32))
+        own_scr[:, pl.ds(pl.multiple_of(j * CB, CB), CB)] = mine.astype(BF16)
+        return t_sum
+
+    balance(t2, uh_ref, gain, scr, acc, None, finish, 0)
+    t_sum = mm(own_scr[...], uh_ref[...], 1, 1)
     pay[0:n_t, :] = lane_sums(acc, n_t)
     pay[n_t : n_t + 2 * th, :] = t_sum
     pay[n_t + 2 * th :, :] = total_of(ex2, n_t, 16)
@@ -426,7 +428,7 @@
         t2,
         half,
         token,
-        scratch=big + [pltpu.VMEM((teachers, 128), F32)],
+        scratch=big + [pltpu.VMEM((teachers, 128), F32), pltpu.VMEM((teach, cols), BF16)],
         flops=fl // 4,
     )
     ex3 = lax.all_gather(pay3, ("y", "c"))

time: 163 us -> 163 us (level)
    all_to_all x2, waiting for transfers between devices: 10.3 us -> 12 us  [swap(): return lax.all_to_all(x, axes, 0, 0, tiled=True)]
    pallas_call x9, Pallas kernels: 44.6 us -> 43 us  [call(): pl.pallas_call(kernel, out_shape=out_shape, in_specs=[specs] * len(args),...]
  transfers between devices with their start and end apart: 3 -> 3, of which waited for: 3 -> 3; matrix products, arithmetic and copies ran while one was open for 0% -> 0% of each run, Pallas kernels for 15% -> 14%
where the time goes in v6:
time: 163 us; the launch traced here: 162 us
  blocking collectives  80.6 us (49%)
  Pallas kernels  43 us (26%)
  starting transfers between devices  23.5 us (14%)
  waiting for transfers between devices  13.5 us (8%)
    all_to_all x3, blocking collectives, swap(): return lax.all_to_all(x, axes, 0, 0, tiled=True)  64.7 us
    pallas_call x9, Pallas kernels, call(): pl.pallas_call(kernel, out_shape=out_shape, in_specs=[specs] * len(args),...  43 us
    all_gather x1, blocking collectives, per_device(): ex3 = lax.all_gather(pay3, ('y', 'c'))  15.9 us
    all_to_all x2, starting transfers between devices, swap(): return lax.all_to_all(x, axes, 0, 0, tiled=True)  14 us
    all_to_all x2, waiting for transfers between devices, swap(): return lax.all_to_all(x, axes, 0, 0, tiled=True)  12 us
    ppermute x1, starting transfers between devices, per_device(): other = lax.ppermute(near, 'c', [(0, 1), (1, 0)])  9.51 us
  transfers between devices with their start and end apart: 3, of which 3 were waited for; matrix products, arithmetic and copies ran while one was open for 0% of the time, Pallas kernels for 14%

profile of v6, /device:TPU:1, one launch (start us, length us, event | category | flops | bytes accessed | tf_op | source)
XLA Modules:
  0.0 162.2 jit_solution(9977235422484695547)
XLA Ops:
  0.6 1.7 %shard_map.68 = f32[16,32,128]{2,1,0:T(8,128)} custom-call(bf16[160,128]{1,0:T(8,128)(2,1)} %student.5, bf16[32,128]{1,0:T(8,128)(2,1)} %teacher.1, s32[1,160]{1,0:T(1,128)} %bitcast.5, s32[1,160]{1,0:T(1,128)} %bitcast.7), custom_call_target="tpu_custom_call" | custom-call | tf_op jit(solution)/shard_map/pallas_call | solution.py:34
  2.4 32.5 %all_to_all.25.got = f32[16,32,128]{2,1,0:T(8,128)S(1)} all-to-all(f32[16,32,128]{2,1,0:T(8,128)} %shard_map.68), channel_id=1, replica_groups=mesh['z'=16,'x'=4,'y'=8,'c'=2] {'z'}, dimensions={0} | all-to-all | bytes 524288 | tf_op jit(solution)/shard_map/all_to_all | solution.py:350
  34.9 0.0 copy-start
  34.9 0.8 copy-done
  35.7 0.1 shard_map.69
  35.8 0.0 copy-start.4
  35.8 14.6 %all_to_all.26.near = f32[4,592,128]{2,1,0:T(8,128)S(1)} all-to-all(f32[4,592,128]{2,1,0:T(8,128)S(1)} %shard_map.69), channel_id=1, replica_groups=mesh['z'=16,'x'=4,'y'=8,'c'=2] {'x'}, dimensions={0} | all-to-all | bytes 2424832 | tf_op jit(solution)/shard_map/all_to_all | solution.py:350
  50.4 9.5 %collective-permute-start = (f32[4,592,128]{2,1,0:T(8,128)S(1)}, f32[4,592,128]{2,1,0:T(8,128)S(1)}, u32[]{:S(2)}, u32[]{:S(2)}) collective-permute-start(f32[4,592,128]{2,1,0:T(8,128)S(1)} %all_to_all.26.near), channel_id=1, source_target_pairs={{0,1},{1,0},{2,3},{3,2},{4,5},{5,4},{6,7},{7,6},{8,9},{9,8},{10,11... | collective-permute-start | bytes 3637256 | tf_op jit(solution)/shard_map/ppermute | solution.py:388
  59.9 0.0 copy-done.4
  59.9 0.9 shard_map.70
  60.9 1.5 collective-permute-done.other
  62.4 9.7 %shard_map.71 = (bf16[2048,256]{1,0:T(8,128)(2,1)S(1)}, bf16[640,128]{1,0:T(8,128)(2,1)S(1)}, f32[2048,128]{1,0:T(8,128)S(1)}, f32[160,128]{1,0:T(8,128)S(1)}, f32[16,24,128]{2,1,0:T(8,128)S(1)}) custom-call(f32[4,592,128]{2,1,0:T(8,128)S(1)} %all_to_all.26.near, f32[4,592,128]{2,1,0:T(8,128)S(1)} %collective-permute-done.other, ...), custom_call_target="tpu_custom_call" | custom-call | flops 4294967296 | tf_op jit(solution)/shard_map/pallas_call | solution.py:34
  72.1 0.0 copy-start.5
  72.1 17.6 %all_to_all.27.ex1 = f32[16,24,128]{2,1,0:T(8,128)S(1)} all-to-all(f32[16,24,128]{2,1,0:T(8,128)S(1)} %get-tuple-element.20), channel_id=1, replica_groups=mesh['z'=16,'x'=4,'y'=8,'c'=2] {'y','c'}, dimensions={0} | all-to-all | bytes 393216 | tf_op jit(solution)/shard_map/all_to_all | solution.py:350
  89.7 8.1 %shard_map.72 = (f32[16,32,128]{2,1,0:T(8,128)}, f32[16,128]{1,0:T(8,128)S(1)}) custom-call(f32[16,24,128]{2,1,0:T(8,128)S(1)} %all_to_all.27.ex1, f32[160,128]{1,0:T(8,128)S(1)} %get-tuple-element.22.e1, bf16[2048,256]{1,0:T(8,128)(2,1)S(1)} %get-tuple-element.23.t2, bf16[128,4096]{1,0:T(8,128)(2,1)S(1)} %get-tuple-element.19.uh_ref), custom_call_target="tpu_custom_call" | custom-call | flops 1073741824 | tf_op jit(solution)/shard_map/pallas_call | solution.py:34
  97.8 0.0 copy-done.5
  97.8 3.4 %all-to-all-start.4 = ((f32[16,32,128]{2,1,0:T(8,128)}), f32[16,32,128]{2,1,0:T(8,128)S(1)}, u32[]{:S(2)}, u32[]{:S(2)}) async-start(f32[16,32,128]{2,1,0:T(8,128)} %get-tuple-element.26), calls=%async_computation.4 | async-start | bytes 524288 | tf_op jit(solution)/shard_map/all_to_all | solution.py:350
  101.3 5.7 %shard_map.73 = (f32[1536,128]{1,0:T(8,128)}, f32[8,128]{1,0:T(8,128)S(1)}) custom-call(f32[16,24,128]{2,1,0:T(8,128)S(1)} %all_to_all.27.ex1, bf16[640,128]{1,0:T(8,128)(2,1)S(1)} %get-tuple-element.21.s_half, bf16[128,4096]{1,0:T(8,128)(2,1)S(1)} %get-tuple-element.19.uh_ref, f32[16,128]{1,0:T(8,128)S(1)} %get-tuple-element.24.log_a1), custom_call_target="tpu_custom_call" | custom-call | flops 2147483648 | tf_op jit(solution)/shard_map/pallas_call | solution.py:34
  107.0 5.6 %all-to-all-done.4.ex2 = f32[16,32,128]{2,1,0:T(8,128)S(1)} async-done(((f32[16,32,128]{2,1,0:T(8,128)}), f32[16,32,128]{2,1,0:T(8,128)S(1)}, u32[]{:S(2)}, u32[]{:S(2)}) %all-to-all-start.4) | async-done | bytes 262176 | tf_op jit(solution)/shard_map/all_to_all | solution.py:350
  112.7 10.5 %all-to-all-start.3 = ((f32[16,96,128]{2,1,0:T(8,128)}), f32[16,96,128]{2,1,0:T(8,128)S(1)}, u32[]{:S(2)}, u32[]{:S(2)}) async-start(f32[16,96,128]{2,1,0:T(8,128)} %bitcast.2), calls=%async_computation.3 | async-start | bytes 1572864 | tf_op jit(solution)/shard_map/all_to_all | solution.py:350
  123.2 0.0 copy-start.1
  123.2 0.0 copy-start.2
  123.2 0.0 copy-start.3
  123.2 0.0 copy-start.6
  123.2 7.6 %shard_map.74 = (f32[64,128]{1,0:T(8,128)S(1)}, f32[16,128]{1,0:T(8,128)S(1)}, f32[1,4096]{1,0:T(1,128)S(1)}) custom-call(f32[16,32,128]{2,1,0:T(8,128)S(1)} %all-to-all-done.4.ex2, f32[16,128]{1,0:T(8,128)S(1)} %get-tuple-element.24.log_a1, bf16[2048,256]{1,0:T(8,128)(2,1)S(1)} %get-tuple-element.23.t2, bf16[128,4096]{1,0:T(8,128)(2,1)S(1)} %get-tuple-element.19.uh_ref, ...), custom_call_target="tpu_custom_call" | custom-call | flops 1073741824 | tf_op jit(solution)/shard_map/pallas_call | solution.py:34
  130.9 15.9 %all-gather = f32[1024,128]{1,0:T(8,128)S(1)} all-gather(f32[64,128]{1,0:T(8,128)S(1)} %get-tuple-element.28), channel_id=2, replica_groups=mesh['z'=16,'x'=4,'y'=8,'c'=2] {'y','c'}, dimensions={0}, use_global_device_ids=true | all-gather | bytes 557056 | tf_op jit(solution)/shard_map/all_gather | solution.py:434
  146.8 0.0 copy-done.1
  146.8 0.0 copy-done.2
  146.8 0.0 copy-done.3
  146.8 0.0 copy-done.6
  146.8 8.3 %shard_map.75 = (f32[3,4096]{1,0:T(4,128)S(1)}, f32[160,128]{1,0:T(8,128)}) custom-call(f32[16,64,128]{2,1,0:T(8,128)S(1)} %bitcast.4, f32[16,128]{1,0:T(8,128)S(1)} %get-tuple-element.29.log_a2, f32[1,4096]{1,0:T(1,128)S(1)} %get-tuple-element.30.b_ref, bf16[2048,256]{1,0:T(8,128)(2,1)S(1)} %get-tuple-element.23.t2, ...), custom_call_target="tpu_custom_call" | custom-call | flops 8589934592 | tf_op jit(solution)/shard_map/pallas_call | solution.py:34
  155.1 6.3 %all-to-all-done.3.d1 = f32[16,96,128]{2,1,0:T(8,128)S(1)} async-done(((f32[16,96,128]{2,1,0:T(8,128)}), f32[16,96,128]{2,1,0:T(8,128)S(1)}, u32[]{:S(2)}, u32[]{:S(2)}) %all-to-all-start.3) | async-done | bytes 786464 | tf_op jit(solution)/shard_map/all_to_all | solution.py:350
  161.4 0.7 shard_map.76
Async XLA Ops:
  34.9 0.8 copy-start
  35.8 24.1 %copy-start.4 = (f32[128,4096]{1,0:T(8,128)S(1)}, f32[128,4096]{1,0:T(8,128)}, u32[]{:S(2)}) copy-start(f32[128,4096]{1,0:T(8,128)} %proto.1) | copy-start | bytes 6291460
  50.4 12.0 %collective-permute-start = (f32[4,592,128]{2,1,0:T(8,128)S(1)}, f32[4,592,128]{2,1,0:T(8,128)S(1)}, u32[]{:S(2)}, u32[]{:S(2)}) collective-permute-start(f32[4,592,128]{2,1,0:T(8,128)S(1)} %all_to_all.26.near), channel_id=1, source_target_pairs={{0,1},{1,0},{2,3},{3,2},{4,5},{5,4},{6,7},{7,6},{8,9},{9,8},{10,11... | collective-permute-start | bytes 3637256 | tf_op jit(solution)/shard_map/ppermute | solution.py:388
  72.1 25.7 %copy-start.5 = (f32[2048,128]{1,0:T(8,128)}, f32[2048,128]{1,0:T(8,128)S(1)}, u32[]{:S(2)}) copy-start(f32[2048,128]{1,0:T(8,128)S(1)} %get-tuple-element.31.mixed) | copy-start | bytes 3145732
  97.8 14.8 %all-to-all-start.4 = ((f32[16,32,128]{2,1,0:T(8,128)}), f32[16,32,128]{2,1,0:T(8,128)S(1)}, u32[]{:S(2)}, u32[]{:S(2)}) async-start(f32[16,32,128]{2,1,0:T(8,128)} %get-tuple-element.26), calls=%async_computation.4 | async-start | bytes 524288 | tf_op jit(solution)/shard_map/all_to_all | solution.py:350
  112.7 48.8 %all-to-all-start.3 = ((f32[16,96,128]{2,1,0:T(8,128)}), f32[16,96,128]{2,1,0:T(8,128)S(1)}, u32[]{:S(2)}, u32[]{:S(2)}) async-start(f32[16,96,128]{2,1,0:T(8,128)} %bitcast.2), calls=%async_computation.3 | async-start | bytes 1572864 | tf_op jit(solution)/shard_map/all_to_all | solution.py:350
  123.2 23.6 %copy-start.1 = (bf16[160,128]{1,0:T(8,128)(2,1)S(1)}, bf16[160,128]{1,0:T(8,128)(2,1)}, u32[]{:S(2)}) copy-start(bf16[160,128]{1,0:T(8,128)(2,1)} %student.5) | copy-start | bytes 122884
  123.2 23.6 %copy-start.2 = (s32[160]{0:T(256)S(1)}, s32[160]{0:T(256)}, u32[]{:S(2)}) copy-start(s32[160]{0:T(256)} %param.8) | copy-start | bytes 1924
  123.2 23.6 %copy-start.3 = (s32[160]{0:T(256)S(1)}, s32[160]{0:T(256)}, u32[]{:S(2)}) copy-start(s32[160]{0:T(256)} %param.9) | copy-start | bytes 1924
  123.2 23.6 %copy-start.6 = (f32[2048,128]{1,0:T(8,128)S(1)}, f32[2048,128]{1,0:T(8,128)}, u32[]{:S(2)}) copy-start(f32[2048,128]{1,0:T(8,128)} %copy-done.5) | copy-start | bytes 3145732
